TPU v7x, 32 devices: a whole 2x2x4 slice. The times are simulated.
32 devices in a mesh: groups: 2 (over y), space: 8 (over z, x), seg: 2 (over core).
Axes of the slice: x: 2, y: 2, z: 4, core: 2. Of those that a mesh axis runs over, the one named last changes fastest.
Arguments:
- modes: bfloat16 [8, 32, 128, 128], P(None, 'space'), may hold values from -0.1 to 0.1
- states: float32 [32, 8, 32, 128], P(('groups', 'seg'), None, 'space'), parts along dimension 0, may hold values from -6 to 6
- lift_one: bfloat16 [64, 8], replicated, may hold values from -2 to 2
- kern_one: float32 [64, 9], replicated, may hold values from -2 to 2
- bias_one: float32 [64], replicated, may hold values from -3 to 3
- proj_one: bfloat16 [8, 64], replicated, may hold values from -0.75 to 0.75
- lift_two: bfloat16 [64, 8], replicated, may hold values from -2 to 2
- kern_two: float32 [64, 9], replicated, may hold values from -2 to 2
- bias_two: float32 [64], replicated, may hold values from -3 to 3
- proj_two: bfloat16 [8, 64], replicated, may hold values from -0.75 to 0.75
Outputs:
- advanced: float32 [32, 8, 32, 128], P(('groups', 'seg'), None, 'space'), parts along dimension 0
- coeffs: float32 [32, 128], P(('groups', 'seg')), parts along dimension 0
There are 2 independent parts, one for each index of `groups`. A program takes and returns all parts, laid end to end along the dimension named above; an argument that names none is the same for every part. Nothing has to cross between parts.
All inputs are finite; a program needn't handle non-finite values.
Results may differ from a plain program's by a relative error of at most 0.0033.
Values may be sent and summed in bfloat16 or wider, within the bound.
A program may use at most 320 MiB of HBM per device.

v0:
```python
import jax
import jax.numpy as jnp
from jax import lax
from jax.sharding import PartitionSpec as P

HI = lax.Precision.HIGHEST


def extended_2(cells, sides, width):
    for axis, dim in sides:
        count = lax.axis_size(axis)
        ends = count - 1
        head = lax.slice_in_dim(cells, 0, width, axis=dim)
        tail = lax.slice_in_dim(cells, cells.shape[dim] - width, cells.shape[dim], axis=dim)
        cells = jnp.concatenate(
            [
                lax.ppermute(tail, axis, [(i, (i + 1) % count) for i in range(ends)]),
                cells,
                lax.ppermute(head, axis, [((i + 1) % count, i) for i in range(ends)]),
            ],
            axis=dim,
        )
    return cells


def passed_along(value, axis, steps):
    count = lax.axis_size(axis)
    leading, last = (max(0, -steps), min(count, count - steps))
    return lax.ppermute(value, axis, [(source, source + steps) for source in range(leading, last)])


def entering(value, axis, join, neutral):
    count, mine = (lax.axis_size(axis), lax.axis_index(axis))
    pieces = jax.tree.map(lambda part: lax.all_gather(part, axis), value)
    total = jax.tree.map(
        lambda part, zero: jnp.full_like(part, 0) + jnp.asarray(zero, part.dtype), value, neutral
    )

    def turn(position, total):
        longer = join(total, jax.tree.map(lambda part: part[position], pieces))
        return jax.tree.map(lambda new, old: jnp.where(position < mine, new, old), longer, total)

    return lax.fori_loop(0, count - 1, turn, total)


def depthwise_valid(z, kern):
    r, w = (z.shape[1] - 2, z.shape[2])
    pads = [(0, 0), (0, 0), (1, 1)] + [(0, 0)] * (z.ndim - 3)
    padded = jnp.pad(z, pads)
    total = jnp.zeros((z.shape[0], r) + z.shape[2:], jnp.float32)
    for i in range(3):
        for j in range(3):
            weight = kern[:, 3 * i + j].reshape((-1,) + (1,) * (z.ndim - 1))
            total = total + weight * padded[:, i : i + r, j : j + w]
    return total


def inside(count, offset, rows):
    glob = lax.axis_index("space") * rows + offset + jnp.arange(count)
    return ((glob >= 0) & (glob < rows * lax.axis_size("space"))).astype(jnp.float32)


def join_maps(earlier, later):
    first_mat, first_vec = earlier
    second_mat, second_vec = later
    return (
        jnp.dot(second_mat, first_mat, precision=HI),
        jnp.dot(second_mat, first_vec, precision=HI) + second_vec,
    )


def on_device(
    modes, states, lift_one, kern_one, bias_one, proj_one, lift_two, kern_two, bias_two, proj_two
):
    fields, rows, cols, nmodes = modes.shape
    seg_count = states.shape[0]
    channels = lift_one.shape[0]
    width = min(8, channels)
    blocks = channels // width
    spread = extended_2(states, (("space", 2),), 2)
    follow = passed_along(states[0], "seg", -1)
    advanced = []
    slopes_one = []
    slopes_two = []
    defects = []
    for seg in range(seg_count):
        extended = spread[seg]
        lifted = jnp.einsum("cf,frw->crw", lift_one.astype(jnp.float32), extended, precision=HI)
        act_one = jnp.tanh(depthwise_valid(lifted, kern_one) + bias_one[:, None, None])
        middle = extended[:, 1:-1] + jnp.einsum(
            "fc,crw->frw", proj_one.astype(jnp.float32), act_one, precision=HI
        )
        middle = middle * inside(rows + 2, -1, rows)[None, :, None]
        lifted_two = jnp.einsum("cf,frw->crw", lift_two.astype(jnp.float32), middle, precision=HI)
        act_two = jnp.tanh(depthwise_valid(lifted_two, kern_two) + bias_two[:, None, None])
        final = middle[:, 1:-1] + jnp.einsum(
            "fc,crw->frw", proj_two.astype(jnp.float32), act_two, precision=HI
        )
        advanced.append(final)
        slope = 1.0 - act_one * act_one
        slopes_one.append(slope[:, 1:-1])
        slopes_two.append(1.0 - act_two * act_two)
        target = states[seg + 1] if seg + 1 < seg_count else follow
        defects.append((final - target).astype(jnp.bfloat16))
    base = extended_2(modes, (("space", 1),), 1)
    totals = [jnp.zeros((fields, rows, cols, nmodes), jnp.float32) for seg in range(seg_count)]
    for blk in range(blocks):
        low = blk * width
        lifted = jnp.einsum(
            "cf,frwk->crwk", lift_one[low : low + width], base, preferred_element_type=jnp.float32
        )
        spatial = depthwise_valid(lifted, kern_one[low : low + width])
        for seg in range(seg_count):
            scaled = (slopes_one[seg][low : low + width][..., None] * spatial).astype(jnp.bfloat16)
            totals[seg] = totals[seg] + jnp.einsum(
                "fc,crwk->frwk",
                proj_one[:, low : low + width],
                scaled,
                preferred_element_type=jnp.float32,
            )
    mats = []
    vecs = []
    for seg in range(seg_count):
        first = (modes.astype(jnp.float32) + totals[seg]).astype(jnp.bfloat16)
        first = extended_2(first, (("space", 1),), 1)
        summed = jnp.zeros((fields, rows, cols, nmodes), jnp.float32)
        for blk in range(blocks):
            low = blk * width
            lifted = jnp.einsum(
                "cf,frwk->crwk",
                lift_two[low : low + width],
                first,
                preferred_element_type=jnp.float32,
            )
            spatial = depthwise_valid(lifted, kern_two[low : low + width])
            scaled = (slopes_two[seg][low : low + width][..., None] * spatial).astype(jnp.bfloat16)
            summed = summed + jnp.einsum(
                "fc,crwk->frwk",
                proj_two[:, low : low + width],
                scaled,
                preferred_element_type=jnp.float32,
            )
        tangent = (first[:, 1:-1].astype(jnp.float32) + summed).astype(jnp.bfloat16)
        mats.append(jnp.einsum("frwi,frwj->ij", modes, tangent, preferred_element_type=jnp.float32))
        vecs.append(
            jnp.einsum("frwk,frw->k", modes, defects[seg], preferred_element_type=jnp.float32)
        )
    mats = jnp.stack(mats)
    vecs = jnp.stack(vecs)
    coeffs = []
    mats, vecs = lax.psum((mats, vecs), "space")
    whole_mat = jnp.eye(nmodes, dtype=jnp.float32)
    whole_vec = jnp.zeros((nmodes,), jnp.float32)
    for seg in range(seg_count):
        whole_mat, whole_vec = join_maps((whole_mat, whole_vec), (mats[seg], vecs[seg]))
    identity = (jnp.eye(nmodes, dtype=jnp.float32), jnp.zeros((nmodes,), jnp.float32))
    before = entering((whole_mat, whole_vec), "seg", join_maps, identity)
    current = before[1]
    for seg in range(seg_count):
        coeffs.append(current)
        current = jnp.dot(mats[seg], current, precision=HI) + vecs[seg]
    return (jnp.stack(advanced), jnp.stack(coeffs))


def solution(mesh):
    placed = (
        P(None, "space", None, None),
        P(("groups", "seg"), None, "space", None),
        P(),
        P(),
        P(),
        P(),
        P(),
        P(),
        P(),
        P(),
    )
    return jax.shard_map(
        on_device,
        mesh=mesh,
        in_specs=placed,
        out_specs=(P(("groups", "seg"), None, "space", None), P(("groups", "seg"), None)),
        check_vma=False,
    )
```

profile of v0, /device:TPU:31, one launch (start us, length us, event | category | flops | bytes accessed | tf_op | source)
XLA Modules:
  0.0 865.4 jit_solution(18276772778301785860)
XLA Ops:
  9.5 4.0 collective-permute-start.1
  17.8 4.7 collective-permute-start.3
  23.1 4.3 collective-permute-start.20
  197.8 4.1 fusion.1136
  218.7 4.1 fusion.1137
  223.7 4.0 collective-permute-start.7
  240.6 4.1 fusion.1138
  258.8 4.5 fusion.1139
  276.0 4.5 fusion.1140
  293.4 4.5 fusion.1141
  325.2 3.4 fusion.1142
  328.7 4.9 fusion.1143
  335.3 4.0 collective-permute-start.9
  341.7 3.4 fusion.1580
  345.1 4.3 collective-permute-start.11
  351.6 3.8 fusion.1566
  356.4 3.4 fusion.1582
  365.2 3.4 fusion.1584
  373.9 3.4 fusion.1586
  382.7 3.4 fusion.1588
  391.4 3.4 fusion.1592
  400.1 3.6 fusion.1590
  404.7 3.4 fusion.1576
  408.1 4.9 collective-permute-start.13
  415.1 3.4 fusion.1552
  419.5 3.4 fusion.1554
  428.2 3.4 fusion.1558
  432.5 3.4 fusion.1560
  441.2 3.4 fusion.1562
  444.6 4.9 collective-permute-start.15
  451.7 3.6 fusion.1538
  456.3 3.4 fusion.1540
  464.9 3.4 fusion.1544
  469.3 3.4 fusion.1546
  473.6 3.4 fusion.1550
  481.3 4.9 collective-permute-start.17
  488.4 3.6 fusion.1524
  493.0 3.4 fusion.1526
  510.3 3.4 fusion.1536
  514.7 3.4 fusion.1534
  518.1 4.9 collective-permute-start.19
  525.2 3.9 fusion.1510
  530.0 3.4 fusion.1512
  543.0 3.4 fusion.1518
  564.7 3.4 fusion.1500
  569.0 3.4 fusion.1502
  577.7 3.5 fusion.1508
  582.2 3.4 fusion.1506
  595.3 3.4 fusion.1486
  599.6 3.4 fusion.1488
  604.0 3.4 fusion.1490
  612.6 3.4 fusion.1492
  618.6 14.4 %fusion.1159 = f32[8,128,128]{1,2,0:T(8,128)} fusion(f32[4,128,128,8]{2,3,1,0:T(8,128)} %fusion.1580, f32[4,128,128,8]{2,3,1,0:T(8,128)} %fusion.1582, f32[4,128,128,8]{2,3,1,0:T(8,128)} %fusion.1584, f32[4,128,128,8]{2,3,1,0:T(8,128)} %fusion.1586, f32[4,128,128,8]{2,3,1,0:T(8,128)} %fusion.1588, f32[4,128,128,8]{2,3,1,0:T(8,128)} %fusion.1592, ...), kind=kOutput, calls=%fused_computation.1991 | convolution fusion | flops 157810688 | bytes 26543392 | tf_op jit(solution)/shard_map/frwi,frwj->ij/dot_general | solution.py:144
  636.3 14.7 %fusion.1158 = f32[8,128,128]{1,2,0:T(8,128)} fusion(f32[8,128,128]{1,2,0:T(8,128)} %fusion.1159, f32[4,128,128,8]{2,3,1,0:T(8,128)} %fusion.1566, f32[4,128,128,8]{2,3,1,0:T(8,128)} %fusion.1568, f32[4,128,128,8]{2,3,1,0:T(8,128)} %fusion.1570, f32[4,128,128,8]{2,3,1,0:T(8,128)} %fusion.1572, f32[4,128,128,8]{2,3,1,0:T(8,128)} %fusion.1574, ...), kind=kOutput, calls=%fused_computation.1989 | convolution fusion | flops 157810688 | bytes 26543392 | tf_op jit(solution)/shard_map/frwi,frwj->ij/dot_general | solution.py:144
  654.4 14.7 %fusion.1157 = f32[8,128,128]{1,2,0:T(8,128)} fusion(f32[8,128,128]{1,2,0:T(8,128)} %fusion.1158, f32[4,128,128,8]{2,3,1,0:T(8,128)} %fusion.1552, f32[4,128,128,8]{2,3,1,0:T(8,128)} %fusion.1554, f32[4,128,128,8]{2,3,1,0:T(8,128)} %fusion.1556, f32[4,128,128,8]{2,3,1,0:T(8,128)} %fusion.1558, f32[4,128,128,8]{2,3,1,0:T(8,128)} %fusion.1560, ...), kind=kOutput, calls=%fused_computation.1987 | convolution fusion | flops 157810688 | bytes 26543392 | tf_op jit(solution)/shard_map/frwi,frwj->ij/dot_general | solution.py:144
  672.5 14.7 %fusion.1156 = f32[8,128,128]{1,2,0:T(8,128)} fusion(f32[8,128,128]{1,2,0:T(8,128)} %fusion.1157, f32[4,128,128,8]{2,3,1,0:T(8,128)} %fusion.1538, f32[4,128,128,8]{2,3,1,0:T(8,128)} %fusion.1540, f32[4,128,128,8]{2,3,1,0:T(8,128)} %fusion.1542, f32[4,128,128,8]{2,3,1,0:T(8,128)} %fusion.1544, f32[4,128,128,8]{2,3,1,0:T(8,128)} %fusion.1546, ...), kind=kOutput, calls=%fused_computation.1985 | convolution fusion | flops 157810688 | bytes 26543392 | tf_op jit(solution)/shard_map/frwi,frwj->ij/dot_general | solution.py:144
  690.5 14.6 %fusion.1155 = f32[8,128,128]{1,2,0:T(8,128)} fusion(f32[8,128,128]{1,2,0:T(8,128)} %fusion.1156, f32[4,128,128,8]{2,3,1,0:T(8,128)} %fusion.1524, f32[4,128,128,8]{2,3,1,0:T(8,128)} %fusion.1526, f32[4,128,128,8]{2,3,1,0:T(8,128)} %fusion.1528, f32[4,128,128,8]{2,3,1,0:T(8,128)} %fusion.1530, f32[4,128,128,8]{2,3,1,0:T(8,128)} %fusion.1532, ...), kind=kOutput, calls=%fused_computation.1983 | convolution fusion | flops 157810688 | bytes 26543392 | tf_op jit(solution)/shard_map/frwi,frwj->ij/dot_general | solution.py:144
  708.4 14.9 %fusion.1154 = f32[8,128,128]{1,2,0:T(8,128)} fusion(f32[8,128,128]{1,2,0:T(8,128)} %fusion.1155, f32[4,128,128,8]{2,3,1,0:T(8,128)} %fusion.1510, f32[4,128,128,8]{2,3,1,0:T(8,128)} %fusion.1512, f32[4,128,128,8]{2,3,1,0:T(8,128)} %fusion.1514, f32[4,128,128,8]{2,3,1,0:T(8,128)} %fusion.1516, f32[4,128,128,8]{2,3,1,0:T(8,128)} %fusion.1518, ...), kind=kOutput, calls=%fused_computation.1981 | convolution fusion | flops 157810688 | bytes 26543392 | tf_op jit(solution)/shard_map/frwi,frwj->ij/dot_general | solution.py:144
  723.3 3.4 convolution_bitcast_fusion.8
  726.7 14.6 %fusion.1153 = f32[8,128,128]{1,2,0:T(8,128)} fusion(f32[8,128,128]{1,2,0:T(8,128)} %fusion.1154, f32[4,128,128,8]{2,3,1,0:T(8,128)} %fusion.1496, f32[4,128,128,8]{2,3,1,0:T(8,128)} %fusion.1498, f32[4,128,128,8]{2,3,1,0:T(8,128)} %fusion.1500, f32[4,128,128,8]{2,3,1,0:T(8,128)} %fusion.1502, f32[4,128,128,8]{2,3,1,0:T(8,128)} %fusion.1504, ...), kind=kOutput, calls=%fused_computation.1979 | convolution fusion | flops 157810688 | bytes 26543392 | tf_op jit(solution)/shard_map/frwi,frwj->ij/dot_general | solution.py:144
  744.7 14.6 %fusion.1152 = f32[8,128,128]{1,2,0:T(8,128)} fusion(f32[8,128,128]{1,2,0:T(8,128)} %fusion.1153, f32[4,128,128,8]{2,3,1,0:T(8,128)} %fusion.1482, f32[4,128,128,8]{2,3,1,0:T(8,128)} %fusion.1484, f32[4,128,128,8]{2,3,1,0:T(8,128)} %fusion.1486, f32[4,128,128,8]{2,3,1,0:T(8,128)} %fusion.1488, f32[4,128,128,8]{2,3,1,0:T(8,128)} %fusion.1490, ...), kind=kOutput, calls=%fused_computation.1977 | convolution fusion | flops 157810688 | bytes 26297632 | tf_op jit(solution)/shard_map/frwi,frwj->ij/dot_general | solution.py:144
  761.4 14.8 %psum.15 = f32[8,128]{1,0:T(8,128)S(1)} all-reduce(f32[8,128]{1,0:T(8,128)S(1)} %stack.134), channel_id=1, replica_groups=mesh['groups'=2,'space'=8,'seg'=2] {'space'}, use_global_device_ids=true, to_apply=%region_1.2 | all-reduce | flops 1024 | bytes 8192 | tf_op jit(solution)/shard_map/psum | solution.py:151
  776.2 58.3 %all-reduce.90.cloned.1.call-done = f32[8,128,128]{1,2,0:T(8,128)} async-done(((f32[8,128,128]{1,2,0:T(8,128)}), f32[8,128,128]{1,2,0:T(8,128)}) %all-reduce.90.cloned.1.call-update) | async-done | bytes 524304 | tf_op jit(solution)/shard_map/psum | solution.py:151
  843.6 4.2 all-gather
  (1163 shorter events, 452.3 us)
Async XLA Ops:
  7.2 26.0 %copy-start.123 = (f32[8,8,4,128]{3,2,1,0:T(4,128)S(1)}, f32[8,8,4,128]{3,2,1,0:T(4,128)}, u32[]{:S(2)}) copy-start(f32[8,8,4,128]{3,2,1,0:T(4,128)} %param.11) | copy-start | bytes 393220
  7.2 20.2 %copy-start.193 = (f32[64,9]{0,1:T(8,128)S(1)}, f32[64,9]{0,1:T(8,128)}, u32[]{:S(2)}) copy-start(f32[64,9]{0,1:T(8,128)} %param.13) | copy-start | bytes 6916
  7.2 23.1 %copy-start.194 = (f32[64,9]{0,1:T(8,128)S(1)}, f32[64,9]{0,1:T(8,128)}, u32[]{:S(2)}) copy-start(f32[64,9]{0,1:T(8,128)} %param.17) | copy-start | bytes 6916
  7.2 26.1 %copy-start.122 = (bf16[64,8]{0,1:T(8,128)(2,1)S(1)}, bf16[64,8]{0,1:T(8,128)(2,1)}, u32[]{:S(2)}) copy-start(bf16[64,8]{0,1:T(8,128)(2,1)} %param.12) | copy-start | bytes 3076
  7.2 827.3 %all-reduce.90.cloned.1.call-start = ((), (), s32[]{:S(2)}) async-start(), calls=%async_computation | async-start | bytes 1048576 | tf_op jit(solution)/shard_map/psum | solution.py:151
  8.2 25.0 %collective-permute-start = (f32[8,8,2,128]{3,1,2,0:T(8,128)S(1)}, f32[8,8,2,128]{3,1,2,0:T(8,128)S(1)}, u32[]{:S(2)}, u32[]{:S(2)}) collective-permute-start(f32[8,8,2,128]{3,1,2,0:T(8,128)S(1)} %get-tuple-element.218), channel_id=1, source_target_pairs={{0,2},{2,4},{4,6},{6,8},{8,10},{10,12},{12,14},{1,3},{3,5},{5,7},{... | collective-permute-start | bytes 196616 | tf_op jit(solution)/shard_map/ppermute | solution.py:17
  9.5 23.7 %collective-permute-start.1 = (f32[8,8,2,128]{3,1,2,0:T(8,128)S(1)}, f32[8,8,2,128]{3,1,2,0:T(8,128)S(1)}, u32[]{:S(2)}, u32[]{:S(2)}) collective-permute-start(f32[8,8,2,128]{3,1,2,0:T(8,128)S(1)} %get-tuple-element.217), channel_id=1, source_target_pairs={{2,0},{4,2},{6,4},{8,6},{10,8},{12,10},{14,12},{3,1},{5,3},{7,5},{... | collective-permute-start | bytes 196616 | tf_op jit(solution)/shard_map/ppermute | solution.py:19
  15.5 20.4 %copy-start.212 = (f32[64]{0:T(128)S(1)}, f32[64]{0:T(128)}, u32[]{:S(2)}) copy-start(f32[64]{0:T(128)} %param.14) | copy-start | bytes 772
  15.5 146.5 %collective-permute-start.2 = (bf16[8,1,128,128]{3,0,2,1:T(8,128)(2,1)}, bf16[8,1,128,128]{3,0,2,1:T(8,128)(2,1)}, u32[]{:S(2)}, u32[]{:S(2)}) collective-permute-start(bf16[8,1,128,128]{3,0,2,1:T(8,128)(2,1)} %copy.470), channel_id=1, source_target_pairs={{0,2},{2,4},{4,6},{6,8},{8,10},{10,12},{12,14},{1,3},{3,5},{5,7},{... | collective-permute-start | bytes 786440 | tf_op jit(solution)/shard_map/ppermute | solution.py:17
  17.8 145.9 %collective-permute-start.3 = (bf16[8,1,128,128]{3,0,2,1:T(8,128)(2,1)}, bf16[8,1,128,128]{3,0,2,1:T(8,128)(2,1)}, u32[]{:S(2)}, u32[]{:S(2)}) collective-permute-start(bf16[8,1,128,128]{3,0,2,1:T(8,128)(2,1)} %copy.471), channel_id=1, source_target_pairs={{2,0},{4,2},{6,4},{8,6},{10,8},{12,10},{14,12},{3,1},{5,3},{7,5},{... | collective-permute-start | bytes 786440 | tf_op jit(solution)/shard_map/ppermute | solution.py:19
  23.1 737.3 %collective-permute-start.20 = (f32[8,4,128]{2,0,1:T(8,128)}, f32[8,4,128]{2,0,1:T(8,128)}, u32[]{:S(2)}, u32[]{:S(2)}) collective-permute-start(f32[8,4,128]{2,0,1:T(8,128)} %slice_bitcast_fusion.39), channel_id=1, source_target_pairs={{1,0},{3,2},{5,4},{7,6},{9,8},{11,10},{13,12},{15,14},{17,16},{19,... | collective-permute-start | bytes 49160 | tf_op jit(solution)/shard_map/ppermute | solution.py:29
  201.8 197.2 %copy-start.2 = (bf16[8,4,128,128]{3,0,2,1:T(8,128)(2,1)}, bf16[8,4,128,128]{3,0,2,1:T(8,128)(2,1)S(1)}, u32[]{:S(2)}) copy-start(bf16[8,4,128,128]{3,0,2,1:T(8,128)(2,1)S(1)} %fusion.1136) | copy-start | bytes 3145732
  202.8 132.5 %collective-permute-start.5 = (bf16[8,1,128,128]{3,0,2,1:T(8,128)(2,1)}, bf16[8,1,128,128]{3,0,2,1:T(8,128)(2,1)S(1)}, u32[]{:S(2)}, u32[]{:S(2)}) collective-permute-start(bf16[8,1,128,128]{3,0,2,1:T(8,128)(2,1)} %get-tuple-element.71), channel_id=1, source_target_pairs={{2,0},{4,2},{6,4},{8,6},{10,8},{12,10},{14,12},{3,1},{5,3},{7,5},{... | collective-permute-start | bytes 786440 | tf_op jit(solution)/shard_map/ppermute | solution.py:19
  206.0 133.2 %collective-permute-start.4 = (bf16[8,1,128,128]{3,0,2,1:T(8,128)(2,1)}, bf16[8,1,128,128]{3,0,2,1:T(8,128)(2,1)S(1)}, u32[]{:S(2)}, u32[]{:S(2)}) collective-permute-start(bf16[8,1,128,128]{3,0,2,1:T(8,128)(2,1)} %get-tuple-element.70), channel_id=1, source_target_pairs={{0,2},{2,4},{4,6},{6,8},{8,10},{10,12},{12,14},{1,3},{3,5},{5,7},{... | collective-permute-start | bytes 786440 | tf_op jit(solution)/shard_map/ppermute | solution.py:17
  222.8 180.9 %copy-start.4 = (bf16[8,4,128,128]{3,0,2,1:T(8,128)(2,1)}, bf16[8,4,128,128]{3,0,2,1:T(8,128)(2,1)S(1)}, u32[]{:S(2)}) copy-start(bf16[8,4,128,128]{3,0,2,1:T(8,128)(2,1)S(1)} %fusion.1137) | copy-start | bytes 3145732
  223.7 121.4 %collective-permute-start.7 = (bf16[8,1,128,128]{3,0,2,1:T(8,128)(2,1)}, bf16[8,1,128,128]{3,0,2,1:T(8,128)(2,1)S(1)}, u32[]{:S(2)}, u32[]{:S(2)}) collective-permute-start(bf16[8,1,128,128]{3,0,2,1:T(8,128)(2,1)} %get-tuple-element.69), channel_id=1, source_target_pairs={{2,0},{4,2},{6,4},{8,6},{10,8},{12,10},{14,12},{3,1},{5,3},{7,5},{... | collective-permute-start | bytes 786440 | tf_op jit(solution)/shard_map/ppermute | solution.py:19
  227.7 121.7 %collective-permute-start.6 = (bf16[8,1,128,128]{3,0,2,1:T(8,128)(2,1)}, bf16[8,1,128,128]{3,0,2,1:T(8,128)(2,1)S(1)}, u32[]{:S(2)}, u32[]{:S(2)}) collective-permute-start(bf16[8,1,128,128]{3,0,2,1:T(8,128)(2,1)} %get-tuple-element.68), channel_id=1, source_target_pairs={{0,2},{2,4},{4,6},{6,8},{8,10},{10,12},{12,14},{1,3},{3,5},{5,7},{... | collective-permute-start | bytes 786440 | tf_op jit(solution)/shard_map/ppermute | solution.py:17
  244.7 195.5 %copy-start.6 = (bf16[8,4,128,128]{3,0,2,1:T(8,128)(2,1)}, bf16[8,4,128,128]{3,0,2,1:T(8,128)(2,1)S(1)}, u32[]{:S(2)}) copy-start(bf16[8,4,128,128]{3,0,2,1:T(8,128)(2,1)S(1)} %fusion.1138) | copy-start | bytes 3145732
  335.3 63.8 %copy-start.24 = (bf16[8,1,128,128]{3,0,2,1:T(8,128)(2,1)}, bf16[8,1,128,128]{3,0,2,1:T(8,128)(2,1)S(1)}, u32[]{:S(2)}) copy-start(bf16[8,1,128,128]{3,0,2,1:T(8,128)(2,1)S(1)} %collective-permute-done.5) | copy-start | bytes 786436
  335.3 72.8 %collective-permute-start.9 = (bf16[8,1,128,128]{3,0,2,1:T(8,128)(2,1)S(1)}, bf16[8,1,128,128]{3,0,2,1:T(8,128)(2,1)S(1)}, u32[]{:S(2)}, u32[]{:S(2)}) collective-permute-start(bf16[8,1,128,128]{3,0,2,1:T(8,128)(2,1)S(1)} %copy-done.192), channel_id=1, source_target_pairs={{2,0},{4,2},{6,4},{8,6},{10,8},{12,10},{14,12},{3,1},{5,3},{7,5},{... | collective-permute-start | bytes 786440 | tf_op jit(solution)/shard_map/ppermute | solution.py:19
  339.3 59.8 %copy-start.26 = (bf16[8,1,128,128]{3,0,2,1:T(8,128)(2,1)}, bf16[8,1,128,128]{3,0,2,1:T(8,128)(2,1)S(1)}, u32[]{:S(2)}) copy-start(bf16[8,1,128,128]{3,0,2,1:T(8,128)(2,1)S(1)} %collective-permute-done.4) | copy-start | bytes 786436
  339.4 73.5 %collective-permute-start.8 = (bf16[8,1,128,128]{3,0,2,1:T(8,128)(2,1)S(1)}, bf16[8,1,128,128]{3,0,2,1:T(8,128)(2,1)S(1)}, u32[]{:S(2)}, u32[]{:S(2)}) collective-permute-start(bf16[8,1,128,128]{3,0,2,1:T(8,128)(2,1)S(1)} %copy-done.191), channel_id=1, source_target_pairs={{0,2},{2,4},{4,6},{6,8},{8,10},{10,12},{12,14},{1,3},{3,5},{5,7},{... | collective-permute-start | bytes 786440 | tf_op jit(solution)/shard_map/ppermute | solution.py:17
  345.1 58.6 %copy-start.28 = (bf16[8,1,128,128]{3,0,2,1:T(8,128)(2,1)}, bf16[8,1,128,128]{3,0,2,1:T(8,128)(2,1)S(1)}, u32[]{:S(2)}) copy-start(bf16[8,1,128,128]{3,0,2,1:T(8,128)(2,1)S(1)} %collective-permute-done.7) | copy-start | bytes 786436
  345.1 99.5 %collective-permute-start.11 = (bf16[8,1,128,128]{3,0,2,1:T(8,128)(2,1)S(1)}, bf16[8,1,128,128]{3,0,2,1:T(8,128)(2,1)S(1)}, u32[]{:S(2)}, u32[]{:S(2)}) collective-permute-start(bf16[8,1,128,128]{3,0,2,1:T(8,128)(2,1)S(1)} %copy-done.190), channel_id=1, source_target_pairs={{2,0},{4,2},{6,4},{8,6},{10,8},{12,10},{14,12},{3,1},{5,3},{7,5},{... | collective-permute-start | bytes 786440 | tf_op jit(solution)/shard_map/ppermute | solution.py:19
  349.5 54.2 %copy-start.30 = (bf16[8,1,128,128]{3,0,2,1:T(8,128)(2,1)}, bf16[8,1,128,128]{3,0,2,1:T(8,128)(2,1)S(1)}, u32[]{:S(2)}) copy-start(bf16[8,1,128,128]{3,0,2,1:T(8,128)(2,1)S(1)} %collective-permute-done.6) | copy-start | bytes 786436
  349.5 100.0 %collective-permute-start.10 = (bf16[8,1,128,128]{3,0,2,1:T(8,128)(2,1)S(1)}, bf16[8,1,128,128]{3,0,2,1:T(8,128)(2,1)S(1)}, u32[]{:S(2)}, u32[]{:S(2)}) collective-permute-start(bf16[8,1,128,128]{3,0,2,1:T(8,128)(2,1)S(1)} %copy-done.189), channel_id=1, source_target_pairs={{0,2},{2,4},{4,6},{6,8},{8,10},{10,12},{12,14},{1,3},{3,5},{5,7},{... | collective-permute-start | bytes 786440 | tf_op jit(solution)/shard_map/ppermute | solution.py:17
  408.1 32.2 %copy-start.31 = (bf16[8,1,128,128]{3,0,2,1:T(8,128)(2,1)}, bf16[8,1,128,128]{3,0,2,1:T(8,128)(2,1)S(1)}, u32[]{:S(2)}) copy-start(bf16[8,1,128,128]{3,0,2,1:T(8,128)(2,1)S(1)} %collective-permute-done.9) | copy-start | bytes 786436
  408.1 73.3 %collective-permute-start.13 = (bf16[8,1,128,128]{3,0,2,1:T(8,128)(2,1)S(1)}, bf16[8,1,128,128]{3,0,2,1:T(8,128)(2,1)S(1)}, u32[]{:S(2)}, u32[]{:S(2)}) collective-permute-start(bf16[8,1,128,128]{3,0,2,1:T(8,128)(2,1)S(1)} %copy-done.188), channel_id=1, source_target_pairs={{2,0},{4,2},{6,4},{8,6},{10,8},{12,10},{14,12},{3,1},{5,3},{7,5},{... | collective-permute-start | bytes 786440 | tf_op jit(solution)/shard_map/ppermute | solution.py:19
  413.0 27.3 %copy-start.35 = (bf16[8,1,128,128]{3,0,2,1:T(8,128)(2,1)}, bf16[8,1,128,128]{3,0,2,1:T(8,128)(2,1)S(1)}, u32[]{:S(2)}) copy-start(bf16[8,1,128,128]{3,0,2,1:T(8,128)(2,1)S(1)} %collective-permute-done.8) | copy-start | bytes 786436
  413.0 73.2 %collective-permute-start.12 = (bf16[8,1,128,128]{3,0,2,1:T(8,128)(2,1)S(1)}, bf16[8,1,128,128]{3,0,2,1:T(8,128)(2,1)S(1)}, u32[]{:S(2)}, u32[]{:S(2)}) collective-permute-start(bf16[8,1,128,128]{3,0,2,1:T(8,128)(2,1)S(1)} %copy-done.186), channel_id=1, source_target_pairs={{0,2},{2,4},{4,6},{6,8},{8,10},{10,12},{12,14},{1,3},{3,5},{5,7},{... | collective-permute-start | bytes 786440 | tf_op jit(solution)/shard_map/ppermute | solution.py:17
  444.6 32.4 %copy-start.33 = (bf16[8,1,128,128]{3,0,2,1:T(8,128)(2,1)}, bf16[8,1,128,128]{3,0,2,1:T(8,128)(2,1)S(1)}, u32[]{:S(2)}) copy-start(bf16[8,1,128,128]{3,0,2,1:T(8,128)(2,1)S(1)} %collective-permute-done.11) | copy-start | bytes 786436
  444.6 73.5 %collective-permute-start.15 = (bf16[8,1,128,128]{3,0,2,1:T(8,128)(2,1)S(1)}, bf16[8,1,128,128]{3,0,2,1:T(8,128)(2,1)S(1)}, u32[]{:S(2)}, u32[]{:S(2)}) collective-permute-start(bf16[8,1,128,128]{3,0,2,1:T(8,128)(2,1)S(1)} %copy-done.184), channel_id=1, source_target_pairs={{2,0},{4,2},{6,4},{8,6},{10,8},{12,10},{14,12},{3,1},{5,3},{7,5},{... | collective-permute-start | bytes 786440 | tf_op jit(solution)/shard_map/ppermute | solution.py:19
  449.5 27.5 %copy-start.36 = (bf16[8,1,128,128]{3,0,2,1:T(8,128)(2,1)}, bf16[8,1,128,128]{3,0,2,1:T(8,128)(2,1)S(1)}, u32[]{:S(2)}) copy-start(bf16[8,1,128,128]{3,0,2,1:T(8,128)(2,1)S(1)} %collective-permute-done.10) | copy-start | bytes 786436
  449.5 73.4 %collective-permute-start.14 = (bf16[8,1,128,128]{3,0,2,1:T(8,128)(2,1)S(1)}, bf16[8,1,128,128]{3,0,2,1:T(8,128)(2,1)S(1)}, u32[]{:S(2)}, u32[]{:S(2)}) collective-permute-start(bf16[8,1,128,128]{3,0,2,1:T(8,128)(2,1)S(1)} %copy-done.183), channel_id=1, source_target_pairs={{0,2},{2,4},{4,6},{6,8},{8,10},{10,12},{12,14},{1,3},{3,5},{5,7},{... | collective-permute-start | bytes 786440 | tf_op jit(solution)/shard_map/ppermute | solution.py:17
  481.3 32.4 %copy-start.37 = (bf16[8,1,128,128]{3,0,2,1:T(8,128)(2,1)}, bf16[8,1,128,128]{3,0,2,1:T(8,128)(2,1)S(1)}, u32[]{:S(2)}) copy-start(bf16[8,1,128,128]{3,0,2,1:T(8,128)(2,1)S(1)} %collective-permute-done.13) | copy-start | bytes 786436
  481.3 73.7 %collective-permute-start.17 = (bf16[8,1,128,128]{3,0,2,1:T(8,128)(2,1)S(1)}, bf16[8,1,128,128]{3,0,2,1:T(8,128)(2,1)S(1)}, u32[]{:S(2)}, u32[]{:S(2)}) collective-permute-start(bf16[8,1,128,128]{3,0,2,1:T(8,128)(2,1)S(1)} %copy-done.187), channel_id=1, source_target_pairs={{2,0},{4,2},{6,4},{8,6},{10,8},{12,10},{14,12},{3,1},{5,3},{7,5},{... | collective-permute-start | bytes 786440 | tf_op jit(solution)/shard_map/ppermute | solution.py:19
  486.3 27.5 %copy-start.39 = (bf16[8,1,128,128]{3,0,2,1:T(8,128)(2,1)}, bf16[8,1,128,128]{3,0,2,1:T(8,128)(2,1)S(1)}, u32[]{:S(2)}) copy-start(bf16[8,1,128,128]{3,0,2,1:T(8,128)(2,1)S(1)} %collective-permute-done.12) | copy-start | bytes 786436
  486.3 68.7 %collective-permute-start.16 = (bf16[8,1,128,128]{3,0,2,1:T(8,128)(2,1)S(1)}, bf16[8,1,128,128]{3,0,2,1:T(8,128)(2,1)S(1)}, u32[]{:S(2)}, u32[]{:S(2)}) collective-permute-start(bf16[8,1,128,128]{3,0,2,1:T(8,128)(2,1)S(1)} %copy-done.185), channel_id=1, source_target_pairs={{0,2},{2,4},{4,6},{6,8},{8,10},{10,12},{12,14},{1,3},{3,5},{5,7},{... | collective-permute-start | bytes 786440 | tf_op jit(solution)/shard_map/ppermute | solution.py:17
  518.1 32.6 %copy-start.40 = (bf16[8,1,128,128]{3,0,2,1:T(8,128)(2,1)}, bf16[8,1,128,128]{3,0,2,1:T(8,128)(2,1)S(1)}, u32[]{:S(2)}) copy-start(bf16[8,1,128,128]{3,0,2,1:T(8,128)(2,1)S(1)} %collective-permute-done.15) | copy-start | bytes 786436
  518.1 67.5 %collective-permute-start.19 = (bf16[8,1,128,128]{3,0,2,1:T(8,128)(2,1)S(1)}, bf16[8,1,128,128]{3,0,2,1:T(8,128)(2,1)S(1)}, u32[]{:S(2)}, u32[]{:S(2)}) collective-permute-start(bf16[8,1,128,128]{3,0,2,1:T(8,128)(2,1)S(1)} %copy-done.182), channel_id=1, source_target_pairs={{2,0},{4,2},{6,4},{8,6},{10,8},{12,10},{14,12},{3,1},{5,3},{7,5},{... | collective-permute-start | bytes 786440 | tf_op jit(solution)/shard_map/ppermute | solution.py:19
  523.0 27.7 %copy-start.42 = (bf16[8,1,128,128]{3,0,2,1:T(8,128)(2,1)}, bf16[8,1,128,128]{3,0,2,1:T(8,128)(2,1)S(1)}, u32[]{:S(2)}) copy-start(bf16[8,1,128,128]{3,0,2,1:T(8,128)(2,1)S(1)} %collective-permute-done.14) | copy-start | bytes 786436
  523.0 62.5 %collective-permute-start.18 = (bf16[8,1,128,128]{3,0,2,1:T(8,128)(2,1)S(1)}, bf16[8,1,128,128]{3,0,2,1:T(8,128)(2,1)S(1)}, u32[]{:S(2)}, u32[]{:S(2)}) collective-permute-start(bf16[8,1,128,128]{3,0,2,1:T(8,128)(2,1)S(1)} %copy-done.181), channel_id=1, source_target_pairs={{0,2},{2,4},{4,6},{6,8},{8,10},{10,12},{12,14},{1,3},{3,5},{5,7},{... | collective-permute-start | bytes 786440 | tf_op jit(solution)/shard_map/ppermute | solution.py:17
  555.0 26.2 %copy-start.43 = (bf16[8,1,128,128]{3,0,2,1:T(8,128)(2,1)}, bf16[8,1,128,128]{3,0,2,1:T(8,128)(2,1)S(1)}, u32[]{:S(2)}) copy-start(bf16[8,1,128,128]{3,0,2,1:T(8,128)(2,1)S(1)} %collective-permute-done.17) | copy-start | bytes 786436
  555.0 26.2 %copy-start.45 = (bf16[8,1,128,128]{3,0,2,1:T(8,128)(2,1)}, bf16[8,1,128,128]{3,0,2,1:T(8,128)(2,1)S(1)}, u32[]{:S(2)}) copy-start(bf16[8,1,128,128]{3,0,2,1:T(8,128)(2,1)S(1)} %collective-permute-done.16) | copy-start | bytes 786436
  585.6 26.1 %copy-start.46 = (bf16[8,1,128,128]{3,0,2,1:T(8,128)(2,1)}, bf16[8,1,128,128]{3,0,2,1:T(8,128)(2,1)S(1)}, u32[]{:S(2)}) copy-start(bf16[8,1,128,128]{3,0,2,1:T(8,128)(2,1)S(1)} %collective-permute-done.19) | copy-start | bytes 786436
  585.6 26.1 %copy-start.48 = (bf16[8,1,128,128]{3,0,2,1:T(8,128)(2,1)}, bf16[8,1,128,128]{3,0,2,1:T(8,128)(2,1)S(1)}, u32[]{:S(2)}) copy-start(bf16[8,1,128,128]{3,0,2,1:T(8,128)(2,1)S(1)} %collective-permute-done.18) | copy-start | bytes 786436
  618.6 14.4 %copy-start.5 = (bf16[8,4,128,128]{3,0,2,1:T(8,128)(2,1)S(1)}, bf16[8,4,128,128]{3,0,2,1:T(8,128)(2,1)}, u32[]{:S(2)}) copy-start(bf16[8,4,128,128]{3,0,2,1:T(8,128)(2,1)} %copy-done.4) | copy-start | bytes 3145732
  618.6 14.4 %copy-start.29 = (bf16[8,1,128,128]{3,0,2,1:T(8,128)(2,1)S(1)}, bf16[8,1,128,128]{3,0,2,1:T(8,128)(2,1)}, u32[]{:S(2)}) copy-start(bf16[8,1,128,128]{3,0,2,1:T(8,128)(2,1)} %copy-done.28) | copy-start | bytes 786436
  636.3 14.7 %copy-start.7 = (bf16[8,4,128,128]{3,0,2,1:T(8,128)(2,1)S(1)}, bf16[8,4,128,128]{3,0,2,1:T(8,128)(2,1)}, u32[]{:S(2)}) copy-start(bf16[8,4,128,128]{3,0,2,1:T(8,128)(2,1)} %copy-done.6) | copy-start | bytes 3145732
  636.3 14.7 %copy-start.32 = (bf16[8,1,128,128]{3,0,2,1:T(8,128)(2,1)S(1)}, bf16[8,1,128,128]{3,0,2,1:T(8,128)(2,1)}, u32[]{:S(2)}) copy-start(bf16[8,1,128,128]{3,0,2,1:T(8,128)(2,1)} %copy-done.31) | copy-start | bytes 786436
  654.4 14.7 %copy-start.10 = (bf16[8,4,128,128]{3,0,2,1:T(8,128)(2,1)S(1)}, bf16[8,4,128,128]{3,0,2,1:T(8,128)(2,1)}, u32[]{:S(2)}) copy-start(bf16[8,4,128,128]{3,0,2,1:T(8,128)(2,1)} %copy-done.8) | copy-start | bytes 3145732
  654.4 14.8 %copy-start.34 = (bf16[8,1,128,128]{3,0,2,1:T(8,128)(2,1)S(1)}, bf16[8,1,128,128]{3,0,2,1:T(8,128)(2,1)}, u32[]{:S(2)}) copy-start(bf16[8,1,128,128]{3,0,2,1:T(8,128)(2,1)} %copy-done.33) | copy-start | bytes 786436
  672.5 14.7 %copy-start.13 = (bf16[8,4,128,128]{3,0,2,1:T(8,128)(2,1)S(1)}, bf16[8,4,128,128]{3,0,2,1:T(8,128)(2,1)}, u32[]{:S(2)}) copy-start(bf16[8,4,128,128]{3,0,2,1:T(8,128)(2,1)} %copy-done.11) | copy-start | bytes 3145732
  672.5 14.7 %copy-start.38 = (bf16[8,1,128,128]{3,0,2,1:T(8,128)(2,1)S(1)}, bf16[8,1,128,128]{3,0,2,1:T(8,128)(2,1)}, u32[]{:S(2)}) copy-start(bf16[8,1,128,128]{3,0,2,1:T(8,128)(2,1)} %copy-done.37) | copy-start | bytes 786436
  690.5 14.6 %copy-start.16 = (bf16[8,4,128,128]{3,0,2,1:T(8,128)(2,1)S(1)}, bf16[8,4,128,128]{3,0,2,1:T(8,128)(2,1)}, u32[]{:S(2)}) copy-start(bf16[8,4,128,128]{3,0,2,1:T(8,128)(2,1)} %copy-done.14) | copy-start | bytes 3145732
  690.5 14.6 %copy-start.41 = (bf16[8,1,128,128]{3,0,2,1:T(8,128)(2,1)S(1)}, bf16[8,1,128,128]{3,0,2,1:T(8,128)(2,1)}, u32[]{:S(2)}) copy-start(bf16[8,1,128,128]{3,0,2,1:T(8,128)(2,1)} %copy-done.40) | copy-start | bytes 786436
  708.4 14.9 %copy-start.22 = (bf16[8,4,128,128]{3,0,2,1:T(8,128)(2,1)S(1)}, bf16[8,4,128,128]{3,0,2,1:T(8,128)(2,1)}, u32[]{:S(2)}) copy-start(bf16[8,4,128,128]{3,0,2,1:T(8,128)(2,1)} %copy-done.20) | copy-start | bytes 3145732
  708.4 14.9 %copy-start.44 = (bf16[8,1,128,128]{3,0,2,1:T(8,128)(2,1)S(1)}, bf16[8,1,128,128]{3,0,2,1:T(8,128)(2,1)}, u32[]{:S(2)}) copy-start(bf16[8,1,128,128]{3,0,2,1:T(8,128)(2,1)} %copy-done.43) | copy-start | bytes 786436
  726.7 14.6 %copy-start.19 = (bf16[8,4,128,128]{3,0,2,1:T(8,128)(2,1)S(1)}, bf16[8,4,128,128]{3,0,2,1:T(8,128)(2,1)}, u32[]{:S(2)}) copy-start(bf16[8,4,128,128]{3,0,2,1:T(8,128)(2,1)} %copy-done.17) | copy-start | bytes 3145732
  726.7 14.6 %copy-start.47 = (bf16[8,1,128,128]{3,0,2,1:T(8,128)(2,1)S(1)}, bf16[8,1,128,128]{3,0,2,1:T(8,128)(2,1)}, u32[]{:S(2)}) copy-start(bf16[8,1,128,128]{3,0,2,1:T(8,128)(2,1)} %copy-done.46) | copy-start | bytes 786436
  744.7 14.7 %copy-start.199 = (bf16[8,4,128,1]{2,0,1,3:T(8,128)(2,1)S(1)}, bf16[8,4,128,1]{2,0,1,3:T(8,128)(2,1)}, u32[]{:S(2)}) copy-start(bf16[8,4,128,1]{2,0,1,3:T(8,128)(2,1)} %get-tuple-element.146) | copy-start | bytes 24580
  744.7 14.9 %copy-start.196 = (f32[8,8,4,128]{3,1,2,0:T(8,128)S(1)}, f32[8,8,4,128]{3,1,2,0:T(8,128)}, u32[]{:S(2)}) copy-start(f32[8,8,4,128]{3,1,2,0:T(8,128)} %get-tuple-element.411) | copy-start | bytes 393220
  744.7 15.6 %copy-start.211 = (f32[8,4,128]{2,0,1:T(8,128)S(1)}, f32[8,4,128]{2,0,1:T(8,128)}, u32[]{:S(2)}) copy-start(f32[8,4,128]{2,0,1:T(8,128)} %get-tuple-element.412) | copy-start | bytes 49156
  834.5 19.3 %copy-start.59 = (f32[8,128,128]{1,2,0:T(8,128)S(1)}, f32[8,128,128]{1,2,0:T(8,128)}, u32[]{:S(2)}) copy-start(f32[8,128,128]{1,2,0:T(8,128)} %all-reduce.90.cloned.1.call-done) | copy-start | bytes 1572868
  (321 other events, 741.1 us)
Sparse Core Ops, SparseCore 0:
  759.5 74.9 all-reduce.89
where the time goes:
time: 881 us; the launch traced here: 865 us
  matrix products  537 us (61%)
  local copies, waits for them, and re-layouts  146 us (17%)
  starting transfers between devices  62.2 us (7%)
  waiting for transfers between devices  58.4 us (7%)
  other arithmetic  20.9 us (2%)
  blocking collectives  20.8 us (2%)
  between operations  19.3 us (2%)
    dot_general x56, matrix products, on_device(): jnp.einsum('fc,crwk->frwk', proj_two[:, low:low + width], scaled, preferr...  191 us
    dot_general x64, matrix products, on_device(): jnp.einsum('fc,crwk->frwk', proj_one[:, low:low + width], scaled, preferr...  130 us
    dot_general x8, matrix products, on_device(): jnp.einsum('frwi,frwj->ij', modes, tangent, preferred_element_type=jnp.fl...  117 us
    dot_general x64, matrix products, on_device(): jnp.einsum('cf,frwk->crwk', lift_two[low:low + width], first, preferred_e...  63.6 us
    psum x1, waiting for transfers between devices, on_device(): mats, vecs = lax.psum((mats, vecs), 'space')  58.3 us
    slice x68, local copies, waits for them, and re-layouts, on_device(): slopes_one[seg][low:low + width][..., None] * spatial  54.8 us
    slice x68, local copies, waits for them, and re-layouts, on_device(): slopes_two[seg][low:low + width][..., None] * spatial  54.5 us
    ppermute x10, starting transfers between devices, extended_2(): lax.ppermute(head, axis, [((i + 1) % count, i) for i in range(ends)])  43.8 us
  transfers between devices with their start and end apart: 22, of which 1 were waited for; matrix products, arithmetic and copies ran while one was open for 77% of the time, Pallas kernels for 0%

commit v1 on v0

v1 whole, which is shorter than its diff:
```python
import functools

import jax
import jax.numpy as jnp
import numpy as np
from jax import lax
from jax.experimental import pallas as pl
from jax.experimental.pallas import tpu as pltpu
from jax.sharding import PartitionSpec as P

HI = lax.Precision.HIGHEST
F32 = jnp.float32
BF16 = jnp.bfloat16


def dot(a, b):
    return jnp.dot(a, b, preferred_element_type=F32)


def dot_split(x, weight):
    high = x.astype(BF16)
    low = (x - high.astype(F32)).astype(BF16)
    return dot(high, weight) + dot(low, weight)


def regroup(x):
    x = x.reshape(4, 4, 8, 64)
    return jnp.concatenate([x[:, a] for a in range(4)], axis=-1)


def advance_kernel(
    rows, mask_ref, u_ref, l1, l2, p1, p2, k1, k2, b1, b2, s1_ref, s2_ref, out_ref, z_ref, z2_ref, m_ref
):
    span = u_ref.shape[1]
    edge1 = jnp.zeros((rows + 4, 8, z_ref.shape[2]), F32)
    edge2 = jnp.zeros((rows + 2, 8, z_ref.shape[2]), F32)
    z_ref[:, 0:8, :] = edge1
    z_ref[:, span + 8 : span + 16, :] = edge1
    z2_ref[:, 0:8, :] = edge2
    z2_ref[:, span + 8 : span + 16, :] = edge2

    @pl.loop(0, rows + 4)
    def _(r):
        z_ref[r, 8 : span + 8, :] = dot_split(u_ref[r], l1[...])

    pieces = span // 128

    def conv(ref, taps, bias, r, base):
        acc = jnp.broadcast_to(bias[...], (128, taps.shape[1]))
        for i in range(3):
            for j in range(3):
                acc = acc + taps[3 * i + j : 3 * i + j + 1, :] * ref[r + i, pl.ds(base + 8 * j, 128), :]
        return jnp.tanh(acc)

    @pl.loop(0, (rows + 2) * pieces)
    def _(n):
        r, q = n // pieces, n % pieces
        base = pl.multiple_of(q * 128, 128)
        keep = mask_ref[r]
        act = conv(z_ref, k1, b1, r, base)
        s1_ref[r, pl.ds(q * 4, 4)] = regroup((1.0 - act * act) * keep)
        mid = (u_ref[r + 1, pl.ds(base, 128), :] + dot_split(act, p1[...])) * keep
        m_ref[r, pl.ds(base, 128), :] = mid
        z2_ref[r, pl.ds(base + 8, 128), :] = dot_split(mid, l2[...])

    @pl.loop(0, rows * pieces)
    def _(n):
        r, q = n // pieces, n % pieces
        base = pl.multiple_of(q * 128, 128)
        act = conv(z2_ref, k2, b2, r, base)
        s2_ref[r, pl.ds(q * 4, 4)] = regroup(1.0 - act * act)
        out_ref[r, pl.ds(base, 128), :] = m_ref[r + 1, pl.ds(base, 128), :] + dot_split(act, p2[...])


def tangent_kernel(
    rows, segs, low_ref, own_ref, high_ref, turned_ref, s1_ref, s2_ref, pd1, pd2, kern1, kern2, lift1, lift2,
    sel_ref, rep_ref, maps_ref, x_ref, v_ref, t_ref, k1_ref, k2_ref,
):
    span = turned_ref.shape[2]
    tiles = span // 64
    nm = own_ref.shape[2]
    x_ref[0:2] = low_ref[...]
    x_ref[2 : rows + 2] = own_ref[...]
    x_ref[rows + 2 : rows + 4] = high_ref[...]
    v_ref[:, 0:8, :] = jnp.zeros((rows + 2, 8, segs * nm), F32)
    v_ref[:, span + 8 : span + 32, :] = jnp.zeros((rows + 2, 24, segs * nm), F32)
    for kern, lift, k_ref in ((kern1, lift1, k1_ref), (kern2, lift2, k2_ref)):
        wide = jnp.dot(lift[...].astype(F32), rep_ref[...], precision=HI, preferred_element_type=F32)
        for col in range(8):
            taps = jnp.dot(kern[...], sel_ref[col], precision=HI, preferred_element_type=F32)
            k_ref[col // 4, (col % 4) * 64 : (col % 4 + 1) * 64, :] = (taps * wide).astype(BF16)
    maps_ref[...] = jnp.zeros_like(maps_ref)

    def band(slopes, pd, k_ref, h):
        scale = pd[...]
        lhs = jnp.concatenate([(slopes[s : s + 1, :] * scale).astype(BF16) for s in range(segs)], axis=0)
        return dot(lhs, k_ref[h]).astype(BF16)

    @pl.loop(0, (rows + 2) * tiles)
    def _(n):
        r, t = n // tiles, n % tiles
        at = pl.multiple_of(t * 64, 64)
        middle = x_ref[r + 1, pl.ds(at, 80), :]
        near = jnp.concatenate([x_ref[r, pl.ds(at, 80), :], middle, x_ref[r + 2, pl.ds(at, 96), :]], axis=0)
        middle = middle.astype(F32)
        for h in range(2):
            out = dot(band(s1_ref[r, 2 * t + h], pd1, k1_ref, h), near)
            own = middle[8 + 32 * h : 40 + 32 * h]
            for s in range(segs):
                v_ref[r, pl.ds(at + (8 + 32 * h), 32), s * nm : (s + 1) * nm] = own + out[s * 32 : (s + 1) * 32]

    @pl.loop(0, rows)
    def _(r):
        @pl.loop(0, tiles)
        def _(t):
            at = pl.multiple_of(t * 64, 64)
            bands = [band(s2_ref[r, 2 * t + h], pd2, k2_ref, h) for h in range(2)]
            for s in range(segs):
                lanes = slice(s * nm, (s + 1) * nm)
                middle = v_ref[r + 1, pl.ds(at, 80), lanes].astype(BF16)
                near = jnp.concatenate(
                    [
                        v_ref[r, pl.ds(at, 80), lanes].astype(BF16),
                        middle,
                        v_ref[r + 2, pl.ds(at, 96), lanes].astype(BF16),
                    ],
                    axis=0,
                )
                both = jnp.concatenate([b[s * 32 : (s + 1) * 32] for b in bands], axis=0)
                out = dot(both, near) + middle.astype(F32)[8:72]
                t_ref[pl.ds(at, 64), lanes] = out.astype(BF16)

        maps_ref[...] += dot(turned_ref[r], t_ref[...])


def chain_kernel(segs, mats_ref, vecs_ref, start_ref, coeffs_ref, end_ref):
    nm = mats_ref.shape[0]
    current = start_ref[...]
    for s in range(segs):
        coeffs_ref[s : s + 1, :] = current[0:1, :]
        current = (
            lax.dot_general(
                current, mats_ref[:, s * nm : (s + 1) * nm], (((1,), (1,)), ((), ())),
                precision=HI, preferred_element_type=F32,
            )
            + vecs_ref[s : s + 1, :]
        )
    end_ref[...] = current


def selectors():
    sel = np.zeros((8, 9, 256), np.float32)
    rep = np.zeros((8, 256), np.float32)
    for i in range(3):
        for w in range(10):
            for g in range(8):
                lane = 80 * i + 8 * w + g
                rep[g, lane] = 1.0
                for col in range(8):
                    if 0 <= w - col < 3:
                        sel[col, 3 * i + w - col, lane] = 1.0
    return sel, rep


VM = pl.BlockSpec(memory_space=pltpu.VMEM)
SM = pl.BlockSpec(memory_space=pltpu.SMEM)


def on_device(
    modes, states, lift_one, kern_one, bias_one, proj_one, lift_two, kern_two, bias_two, proj_two
):
    fields, rows, cols, nmodes = modes.shape
    segs = states.shape[0]
    channels = lift_one.shape[0]
    count = lax.axis_size("space")
    down = [(i, i + 1) for i in range(count - 1)]
    up = [(i + 1, i) for i in range(count - 1)]

    before = lax.ppermute(states[:, :, rows - 2 :], "space", down)
    after = lax.ppermute(states[:, :, :2], "space", up)
    turns = lax.axis_size("seg")
    follow = lax.ppermute(states[0], "seg", [(i + 1, i) for i in range(turns - 1)])

    own = jnp.transpose(modes, (1, 2, 0, 3)).reshape(rows, cols * fields, nmodes)
    turned = jnp.transpose(own, (0, 2, 1))
    own = jnp.pad(own, ((0, 0), (8, 24), (0, 0)))
    low = lax.ppermute(own[rows - 2 :], "space", down)
    high = lax.ppermute(own[:2], "space", up)

    extended = jnp.concatenate([before, states, after], axis=2)
    u = jnp.transpose(extended, (2, 3, 0, 1)).reshape(rows + 4, cols * segs, fields)
    glob = lax.axis_index("space") * rows - 1 + jnp.arange(rows + 2)
    mask = ((glob >= 0) & (glob < rows * count)).astype(F32)

    groups = cols // 4
    span = cols * segs
    slope_one, slope_two, final = pl.pallas_call(
        functools.partial(advance_kernel, rows),
        out_shape=(
            jax.ShapeDtypeStruct((rows + 2, groups, segs, 4 * channels), F32),
            jax.ShapeDtypeStruct((rows, groups, segs, 4 * channels), F32),
            jax.ShapeDtypeStruct((rows, span, fields), F32),
        ),
        in_specs=[SM] + [VM] * 9,
        out_specs=(VM, VM, VM),
        scratch_shapes=[
            pltpu.VMEM((rows + 4, span + 16, channels), F32),
            pltpu.VMEM((rows + 2, span + 16, channels), F32),
            pltpu.VMEM((rows + 2, span, fields), F32),
        ],
        compiler_params=pltpu.CompilerParams(vmem_limit_bytes=56 * 2**20),
        cost_estimate=pl.CostEstimate(flops=10**8, bytes_accessed=10**7, transcendentals=10**6),
    )(
        mask, u, lift_one.T, lift_two.T, proj_one.T, proj_two.T, kern_one.T, kern_two.T,
        bias_one[None], bias_two[None],
    )
    advanced = jnp.transpose(final.reshape(rows, cols, segs, fields), (2, 3, 0, 1))
    defects = (advanced - jnp.concatenate([states[1:], follow[None]], axis=0)).astype(BF16)
    vecs = jnp.einsum("sfrw,frwk->sk", defects, modes, preferred_element_type=F32)

    sel, rep = selectors()
    blockwise = np.kron(np.eye(4, dtype=np.float32), np.ones((fields, channels), np.float32))
    pd1 = jnp.tile(proj_one.astype(F32), (4, 4)) * blockwise
    pd2 = jnp.tile(proj_two.astype(F32), (4, 4)) * blockwise
    lines = cols * fields
    mats = pl.pallas_call(
        functools.partial(tangent_kernel, rows, segs),
        out_shape=jax.ShapeDtypeStruct((nmodes, segs * nmodes), F32),
        in_specs=[VM] * 14,
        out_specs=VM,
        scratch_shapes=[
            pltpu.VMEM((rows + 4, lines + 32, nmodes), BF16),
            pltpu.VMEM((rows + 2, lines + 32, segs * nmodes), F32),
            pltpu.VMEM((lines, segs * nmodes), BF16),
            pltpu.VMEM((2, 256, 256), BF16),
            pltpu.VMEM((2, 256, 256), BF16),
        ],
        compiler_params=pltpu.CompilerParams(vmem_limit_bytes=56 * 2**20),
        cost_estimate=pl.CostEstimate(flops=2 * 10**10, bytes_accessed=10**7, transcendentals=0),
    )(
        low, own, high, turned, slope_one, slope_two, pd1, pd2, kern_one, kern_two, lift_one, lift_two, sel, rep
    )

    mats, vecs = lax.psum((mats, vecs), "space")
    chain = pl.pallas_call(
        functools.partial(chain_kernel, segs),
        out_shape=(
            jax.ShapeDtypeStruct((segs, nmodes), F32),
            jax.ShapeDtypeStruct((8, nmodes), F32),
        ),
        in_specs=[VM] * 3,
        out_specs=(VM, VM),
    )
    start = jnp.zeros((8, nmodes), F32)
    for _ in range(turns - 1):
        end = chain(mats, vecs, start)[1]
        start = lax.ppermute(end, "seg", [(i, i + 1) for i in range(turns - 1)])
    coeffs = chain(mats, vecs, start)[0]
    return advanced, coeffs


def solution(mesh):
    placed = (
        P(None, "space", None, None),
        P(("groups", "seg"), None, "space", None),
        P(), P(), P(), P(), P(), P(), P(), P(),
    )
    return jax.shard_map(
        on_device,
        mesh=mesh,
        in_specs=placed,
        out_specs=(P(("groups", "seg"), None, "space", None), P(("groups", "seg"), None)),
        check_vma=False,
    )
```

time: 881 us -> 246 us (0.28); the launches traced: 865 us -> 243 us
  matrix products: 537 us -> 0.25 us
  local copies, waits for them, and re-layouts: 146 us -> 15.1 us
  Pallas kernels: 0 us -> 118 us
  starting transfers between devices: 62.2 us -> 13.5 us
  other arithmetic: 20.9 us -> 0.68 us
  waiting for transfers between devices: 58.4 us -> 67.7 us
    dot_general x264 -> x1, matrix products: 537 us -> 0.25 us  [on_device(): jnp.einsum('sfrw,frwk->sk', defects, modes, preferred_element_type=F32)]
    pallas_call x0 -> x4, Pallas kernels: none -> 118 us  [the longest x1 80.8 us: on_device(): pl.pallas_call(functools.partial(tangent_kernel, rows, segs), out_shape=j...]
    slice x146 -> x4, local copies, waits for them, and re-layouts: 118 us -> 0.13 us  [the longest x1 0.07 us: on_device(): high = lax.ppermute(own[:2], 'space', up)]
    ppermute x21 -> x6, starting transfers between devices: 62.2 us -> 13.4 us  [the longest x1 4.79 us: on_device(): high = lax.ppermute(own[:2], 'space', up)]
    ppermute x21 -> x6, waiting for transfers between devices: 0.06 us -> 14.7 us  [the longest x1 11.1 us: on_device(): after = lax.ppermute(states[:, :, :2], 'space', up)]
    add x8 -> x0, other arithmetic: 14.1 us -> none  [depthwise_valid(): total = total + weight * padded[:, i:i + r, j:j + w]]
    unnamed x734 -> x31, local copies, waits for them, and re-layouts: 20.8 us -> 6.69 us
  transfers between devices with their start and end apart: 22 -> 7, of which waited for: 1 -> 4; matrix products, arithmetic and copies ran while one was open for 77% -> 5% of each run, Pallas kernels for 0% -> 12%
where the time goes in v1:
time: 246 us; the launch traced here: 243 us
  Pallas kernels  118 us (48%)
  waiting for transfers between devices  67.7 us (28%)
  local copies, waits for them, and re-layouts  15.1 us (6%)
  blocking collectives  14.2 us (6%)
  between operations  14.2 us (6%)
  starting transfers between devices  13.5 us (5%)
    pallas_call x1, Pallas kernels, on_device(): pl.pallas_call(functools.partial(tangent_kernel, rows, segs), out_shape=j...  80.8 us
    psum x1, waiting for transfers between devices, on_device(): mats, vecs = lax.psum((mats, vecs), 'space')  52.9 us
    pallas_call x1, Pallas kernels, on_device(): pl.pallas_call(functools.partial(advance_kernel, rows), out_shape=(jax.Sh...  28.9 us
    psum x1, blocking collectives, on_device(): mats, vecs = lax.psum((mats, vecs), 'space')  14.2 us
    ppermute x1, waiting for transfers between devices, on_device(): after = lax.ppermute(states[:, :, :2], 'space', up)  11.1 us
    unnamed x31, local copies, waits for them, and re-layouts  6.69 us
  transfers between devices with their start and end apart: 7, of which 4 were waited for; matrix products, arithmetic and copies ran while one was open for 5% of the time, Pallas kernels for 12%

profile of v1, /device:TPU:31, one launch (start us, length us, event | category | flops | bytes accessed | tf_op | source)
XLA Modules:
  0.0 243.1 jit_solution(15835621934728862783)
XLA Ops:
  7.2 0.0 all-reduce.3.cloned.1.call-start
  7.2 1.9 copy.43
  9.1 0.0 copy-start.2
  9.1 0.1 pad_slice_fusion
  9.2 0.0 copy-start.9
  9.2 0.0 copy-start.10
  9.2 1.3 collective-permute-start.2
  10.5 4.8 %collective-permute-start.3 = (bf16[2,1056,128]{2,1,0:T(8,128)(2,1)S(1)}, bf16[2,1056,128]{2,1,0:T(8,128)(2,1)}, u32[]{:S(2)}, u32[]{:S(2)}) collective-permute-start(bf16[2,1056,128]{2,1,0:T(8,128)(2,1)S(1)} %get-tuple-element.12), channel_id=1, source_target_pairs={{2,0},{4,2},{6,4},{8,6},{10,8},{12,10},{14,12},{3,1},{5,3},{7,5},{... | collective-permute-start | bytes 1622024 | tf_op jit(solution)/shard_map/ppermute | solution.py:188
  15.3 0.0 copy-done.2
  15.3 0.1 fusion.2
  15.4 2.3 collective-permute-start.1
  17.7 1.3 collective-permute-start
  19.0 1.3 copy.33
  20.3 0.0 copy-done.9
  20.3 0.0 copy-start.4
  20.3 0.0 copy-start.5
  20.3 0.0 copy-start.6
  20.3 0.0 copy-start.7
  20.3 0.0 copy-start.8
  20.3 0.7 copy.30
  21.0 0.0 copy-done.10
  21.0 0.7 copy.29
  21.7 1.1 pad.4.own_ref
  22.8 0.0 copy-done.4
  22.9 0.7 reshape.19.pd1
  23.6 0.7 reshape.21.pd2
  24.3 0.0 copy-done.5
  24.3 0.7 copy.34.kern1
  25.0 0.0 copy-done.6
  25.0 0.7 copy.35.kern2
  25.7 0.0 copy-done.7
  25.7 0.7 copy.36.lift1
  26.4 0.0 copy-done.8
  26.4 0.7 copy.37.lift2
  27.1 0.5 and_convert_fusion.mask_ref
  27.6 11.1 %collective-permute-done.1 = f32[8,8,2,128]{3,2,1,0:T(2,128)S(1)} collective-permute-done((f32[8,8,2,128]{3,2,1,0:T(2,128)S(1)}, f32[8,8,2,128]{3,2,1,0:T(2,128)S(1)}, u32[]{:S(2)}, u32[]{:S(2)}) %collective-permute-start.1) | collective-permute-done | bytes 65568 | tf_op jit(solution)/shard_map/ppermute | solution.py:180
  38.7 0.0 collective-permute-done
  38.7 0.1 maximum_bitcast_fusion
  38.8 3.1 %copy.28 = f32[8,128,8,8]{3,2,1,0:T(8,128)} copy(f32[8,128,8,8]{1,0,3,2:T(8,128)S(1)} %maximum_bitcast_fusion) | data formatting | bytes 524288 | tf_op jit(solution)/shard_map/transpose | solution.py:191
  41.9 28.9 %shard_map.140 = (f32[6,32,8,256]{3,2,1,0:T(8,128)}, f32[4,32,8,256]{3,2,1,0:T(8,128)}, f32[4,1024,8]{2,1,0:T(8,128)}) custom-call(f32[6]{0:T(128)} %and_convert_fusion.mask_ref, f32[8,1024,8]{2,1,0:T(8,128)} %bitcast.31, bf16[8,64]{1,0:T(8,128)(2,1)} %bitcast.40, bf16[8,64]{1,0:T(8,128)(2,1)} %bitcast.41, bf16[64,8]{1,0:T(8,128)(2,1)} %bitcast.36, ...), custom_call_target="tpu_custom_call" | custom-call | flops 100000000 | bytes 10000000 | tf_op jit(solution)/shard_map/pallas_call | solution.py:197
  70.7 0.0 collective-permute-done.2.low_ref
  70.7 0.0 collective-permute-done.3.high_ref
  70.7 0.0 copy-start.1
  70.7 80.8 %shard_map.141 = f32[128,1024]{1,0:T(8,128)} custom-call(bf16[2,1056,128]{2,1,0:T(8,128)(2,1)} %collective-permute-done.2.low_ref, bf16[4,1056,128]{2,1,0:T(8,128)(2,1)} %pad.4.own_ref, bf16[2,1056,128]{2,1,0:T(8,128)(2,1)} %collective-permute-done.3.high_ref, bf16[4,128,1024]{2,1,0:T(8,128)(2,1)} %bitcast.33, f32[6,32,8,256]{3,2,1,0:T(8,128)} %get-tuple-element.8.s1_ref, ...), custom_call_target="tpu_custom_call" | custom-call | flops 20000000000 | bytes 10000000 | tf_op jit(solution)/shard_map/pallas_call | solution.py:226
  151.6 0.0 slice-start
  151.6 0.0 copy-start
  151.6 0.0 all-reduce.3.cloned.1.call-update
  151.6 2.5 %collective-permute-start.4 = (f32[8,4,128]{2,1,0:T(4,128)S(1)}, f32[8,4,128]{2,1,0:T(4,128)S(1)}, u32[]{:S(2)}, u32[]{:S(2)}) collective-permute-start(f32[8,4,128]{2,1,0:T(4,128)S(1)} %slice_bitcast_fusion), channel_id=1, source_target_pairs={{1,0},{3,2},{5,4},{7,6},{9,8},{11,10},{13,12},{15,14},{17,16},{19,... | collective-permute-start | bytes 49160 | tf_op jit(solution)/shard_map/ppermute | solution.py:182
  154.1 0.0 copy-done.1
  154.1 0.7 copy.31
  154.8 0.0 copy-start.3
  154.8 0.1 collective-permute-done.4
  154.9 0.0 slice-done
  155.0 0.0 copy-done
  155.0 0.2 convolution_bitcast_fusion
  155.3 14.2 %psum.15.vecs_ref = f32[8,128]{1,0:T(8,128)} all-reduce(f32[8,128]{1,0:T(8,128)S(1)} %convolution_bitcast_fusion), channel_id=1, replica_groups=mesh['groups'=2,'space'=8,'seg'=2] {'space'}, use_global_device_ids=true, to_apply=%region_1.2 | all-reduce | flops 1024 | bytes 8192 | tf_op jit(solution)/shard_map/psum | solution.py:244
  169.5 52.9 %all-reduce.3.cloned.1.call-done.mats_ref = f32[128,1024]{1,0:T(8,128)} async-done(((f32[128,1024]{1,0:T(8,128)}), f32[128,1024]{1,0:T(8,128)}) %all-reduce.3.cloned.1.call-update) | async-done | bytes 524304 | tf_op jit(solution)/shard_map/psum | solution.py:244
  222.4 0.6 broadcast_in_dim.15.start_ref
  223.0 4.0 %shard_map.142 = (f32[8,128]{1,0:T(8,128)}, f32[8,128]{1,0:T(8,128)}) custom-call(f32[128,1024]{1,0:T(8,128)} %all-reduce.3.cloned.1.call-done.mats_ref, f32[8,128]{1,0:T(8,128)} %psum.15.vecs_ref, f32[8,128]{1,0:T(8,128)} %broadcast_in_dim.15.start_ref), custom_call_target="tpu_custom_call" | custom-call | tf_op jit(solution)/shard_map/pallas_call | solution.py:256
  226.9 1.3 collective-permute-start.5
  228.2 3.5 %collective-permute-done.5.start_ref = f32[8,128]{1,0:T(8,128)S(1)} collective-permute-done((f32[8,128]{1,0:T(8,128)}, f32[8,128]{1,0:T(8,128)S(1)}, u32[]{:S(2)}, u32[]{:S(2)}) %collective-permute-start.5) | collective-permute-done | bytes 4128 | tf_op jit(solution)/shard_map/ppermute | solution.py:257
  231.7 0.6 copy-done.11
  232.3 4.0 %shard_map.143 = (f32[8,128]{1,0:T(8,128)}, f32[8,128]{1,0:T(8,128)}) custom-call(f32[128,1024]{1,0:T(8,128)} %all-reduce.3.cloned.1.call-done.mats_ref, f32[8,128]{1,0:T(8,128)} %psum.15.vecs_ref, f32[8,128]{1,0:T(8,128)} %copy-done.11), custom_call_target="tpu_custom_call" | custom-call | tf_op jit(solution)/shard_map/pallas_call | solution.py:258
  236.3 0.0 copy-done.3
  (6 shorter events, 0.1 us)
Async XLA Ops:
  7.2 215.2 %all-reduce.3.cloned.1.call-start = ((), (), s32[]{:S(2)}) async-start(), calls=%async_computation | async-start | bytes 1048576 | tf_op jit(solution)/shard_map/psum | solution.py:244
  9.1 6.2 %copy-start.2 = (f32[8,8,4,128]{3,2,1,0:T(4,128)S(1)}, f32[8,8,4,128]{3,2,1,0:T(4,128)}, u32[]{:S(2)}) copy-start(f32[8,8,4,128]{3,2,1,0:T(4,128)} %param.14) | copy-start | bytes 393220
  9.2 11.1 %copy-start.9 = (bf16[8,64]{1,0:T(8,128)(2,1)S(1)}, bf16[8,64]{1,0:T(8,128)(2,1)}, u32[]{:S(2)}) copy-start(bf16[8,64]{1,0:T(8,128)(2,1)} %param.22) | copy-start | bytes 3076
  9.2 11.8 %copy-start.10 = (bf16[8,64]{1,0:T(8,128)(2,1)S(1)}, bf16[8,64]{1,0:T(8,128)(2,1)}, u32[]{:S(2)}) copy-start(bf16[8,64]{1,0:T(8,128)(2,1)} %param.18) | copy-start | bytes 3076
  9.2 61.5 %collective-permute-start.2 = (bf16[2,1056,128]{2,1,0:T(8,128)(2,1)S(1)}, bf16[2,1056,128]{2,1,0:T(8,128)(2,1)}, u32[]{:S(2)}, u32[]{:S(2)}) collective-permute-start(bf16[2,1056,128]{2,1,0:T(8,128)(2,1)S(1)} %get-tuple-element.13), channel_id=1, source_target_pairs={{0,2},{2,4},{4,6},{6,8},{8,10},{10,12},{12,14},{1,3},{3,5},{5,7},{... | collective-permute-start | bytes 1622024 | tf_op jit(solution)/shard_map/ppermute | solution.py:187
  10.5 60.2 %collective-permute-start.3 = (bf16[2,1056,128]{2,1,0:T(8,128)(2,1)S(1)}, bf16[2,1056,128]{2,1,0:T(8,128)(2,1)}, u32[]{:S(2)}, u32[]{:S(2)}) collective-permute-start(bf16[2,1056,128]{2,1,0:T(8,128)(2,1)S(1)} %get-tuple-element.12), channel_id=1, source_target_pairs={{2,0},{4,2},{6,4},{8,6},{10,8},{12,10},{14,12},{3,1},{5,3},{7,5},{... | collective-permute-start | bytes 1622024 | tf_op jit(solution)/shard_map/ppermute | solution.py:188
  15.4 23.3 %collective-permute-start.1 = (f32[8,8,2,128]{3,2,1,0:T(2,128)S(1)}, f32[8,8,2,128]{3,2,1,0:T(2,128)S(1)}, u32[]{:S(2)}, u32[]{:S(2)}) collective-permute-start(f32[8,8,2,128]{3,2,1,0:T(2,128)S(1)} %get-tuple-element.15), channel_id=1, source_target_pairs={{2,0},{4,2},{6,4},{8,6},{10,8},{12,10},{14,12},{3,1},{5,3},{7,5},{... | collective-permute-start | bytes 196616 | tf_op jit(solution)/shard_map/ppermute | solution.py:180
  17.7 21.0 %collective-permute-start = (f32[8,8,2,128]{3,2,1,0:T(2,128)S(1)}, f32[8,8,2,128]{3,2,1,0:T(2,128)S(1)}, u32[]{:S(2)}, u32[]{:S(2)}) collective-permute-start(f32[8,8,2,128]{3,2,1,0:T(2,128)S(1)} %get-tuple-element.14), channel_id=1, source_target_pairs={{0,2},{2,4},{4,6},{6,8},{8,10},{10,12},{12,14},{1,3},{3,5},{5,7},{... | collective-permute-start | bytes 196616 | tf_op jit(solution)/shard_map/ppermute | solution.py:179
  20.3 2.6 %copy-start.4 = (f32[4,8,4,64]{3,2,1,0:T(4,128)S(1)}, f32[4,8,4,64]{3,2,1,0:T(4,128)}, u32[]{:S(2)}) copy-start(f32[4,8,4,64]{3,2,1,0:T(4,128)} %constant.33) | copy-start | bytes 98308
  20.3 4.0 %copy-start.5 = (f32[64,9]{0,1:T(8,128)S(1)}, f32[64,9]{0,1:T(8,128)}, u32[]{:S(2)}) copy-start(f32[64,9]{0,1:T(8,128)} %param.16) | copy-start | bytes 6916
  20.3 4.7 %copy-start.6 = (f32[64,9]{0,1:T(8,128)S(1)}, f32[64,9]{0,1:T(8,128)}, u32[]{:S(2)}) copy-start(f32[64,9]{0,1:T(8,128)} %param.20) | copy-start | bytes 6916
  20.3 5.4 %copy-start.7 = (bf16[64,8]{0,1:T(8,128)(2,1)S(1)}, bf16[64,8]{0,1:T(8,128)(2,1)}, u32[]{:S(2)}) copy-start(bf16[64,8]{0,1:T(8,128)(2,1)} %param.15) | copy-start | bytes 3076
  20.3 6.1 %copy-start.8 = (bf16[64,8]{0,1:T(8,128)(2,1)S(1)}, bf16[64,8]{0,1:T(8,128)(2,1)}, u32[]{:S(2)}) copy-start(bf16[64,8]{0,1:T(8,128)(2,1)} %param.19) | copy-start | bytes 3076
  70.7 83.4 %copy-start.1 = (f32[4,1024,8]{2,1,0:T(8,128)S(1)}, f32[4,1024,8]{2,1,0:T(8,128)}, u32[]{:S(2)}) copy-start(f32[4,1024,8]{2,1,0:T(8,128)} %get-tuple-element.7) | copy-start | bytes 393220
  151.6 3.4 %slice-start = ((f32[8,8,4,128]{3,2,1,0:T(4,128)}), f32[7,8,4,128]{3,2,1,0:T(4,128)S(1)}, s32[]{:S(2)}) async-start(f32[8,8,4,128]{3,2,1,0:T(4,128)} %param.14), calls=%async_computation.1 | async-start | bytes 229376 | tf_op jit(solution)/shard_map/slice | solution.py:218
  151.6 3.4 %copy-start = (bf16[8,4,128,128]{3,2,1,0:T(8,128)(2,1)S(1)}, bf16[8,4,128,128]{3,2,1,0:T(8,128)(2,1)}, u32[]{:S(2)}) copy-start(bf16[8,4,128,128]{3,2,1,0:T(8,128)(2,1)} %param.13) | copy-start | bytes 3145732
  151.6 3.3 %collective-permute-start.4 = (f32[8,4,128]{2,1,0:T(4,128)S(1)}, f32[8,4,128]{2,1,0:T(4,128)S(1)}, u32[]{:S(2)}, u32[]{:S(2)}) collective-permute-start(f32[8,4,128]{2,1,0:T(4,128)S(1)} %slice_bitcast_fusion), channel_id=1, source_target_pairs={{1,0},{3,2},{5,4},{7,6},{9,8},{11,10},{13,12},{15,14},{17,16},{19,... | collective-permute-start | bytes 49160 | tf_op jit(solution)/shard_map/ppermute | solution.py:182
  154.8 81.5 %copy-start.3 = (f32[4,128,8,8]{1,0,3,2:T(4,128)}, f32[4,128,8,8]{1,0,3,2:T(4,128)S(1)}, u32[]{:S(2)}) copy-start(f32[4,128,8,8]{1,0,3,2:T(4,128)S(1)} %copy.31) | copy-start | bytes 393220
  226.9 4.8 %collective-permute-start.5 = (f32[8,128]{1,0:T(8,128)}, f32[8,128]{1,0:T(8,128)S(1)}, u32[]{:S(2)}, u32[]{:S(2)}) collective-permute-start(f32[8,128]{1,0:T(8,128)} %get-tuple-element.10), channel_id=1, source_target_pairs={{0,1},{2,3},{4,5},{6,7},{8,9},{10,11},{12,13},{14,15},{16,17},{18,... | collective-permute-start | bytes 12296 | tf_op jit(solution)/shard_map/ppermute | solution.py:257
  231.7 0.6 copy-start.11
Sparse Core Ops, SparseCore 0:
  151.7 70.6 all-reduce.2

commit v2 on v1

--- a/solution.py
+++ b/solution.py
@@ -17,14 +17,22 @@
     return jnp.dot(a, b, preferred_element_type=F32)
 
 
-def dot_split(x, weight):
+def dot_turned(a, b, side, precision=None):
+    return lax.dot_general(
+        a, b, (((side,), (side,)), ((), ())), precision=precision, preferred_element_type=F32
+    )
+
+
+def dot_split(x, weight, turned=False):
     high = x.astype(BF16)
     low = (x - high.astype(F32)).astype(BF16)
+    if turned:
+        return dot_turned(high, weight, 1) + dot_turned(low, weight, 1)
     return dot(high, weight) + dot(low, weight)
 
 
 def regroup(x):
-    x = x.reshape(4, 4, 8, 64)
+    x = x.reshape(x.shape[0] // 32, 4, 8, x.shape[1])
     return jnp.concatenate([x[:, a] for a in range(4)], axis=-1)
 
 
@@ -43,38 +51,39 @@
     def _(r):
         z_ref[r, 8 : span + 8, :] = dot_split(u_ref[r], l1[...])
 
-    pieces = span // 128
+    size = 256
+    pieces = span // size
 
     def conv(ref, taps, bias, r, base):
-        acc = jnp.broadcast_to(bias[...], (128, taps.shape[1]))
+        acc = jnp.broadcast_to(bias[...], (size, taps.shape[1]))
         for i in range(3):
             for j in range(3):
-                acc = acc + taps[3 * i + j : 3 * i + j + 1, :] * ref[r + i, pl.ds(base + 8 * j, 128), :]
+                acc = acc + taps[3 * i + j : 3 * i + j + 1, :] * ref[r + i, pl.ds(base + 8 * j, size), :]
         return jnp.tanh(acc)
 
     @pl.loop(0, (rows + 2) * pieces)
     def _(n):
         r, q = n // pieces, n % pieces
-        base = pl.multiple_of(q * 128, 128)
+        base = pl.multiple_of(q * size, size)
         keep = mask_ref[r]
         act = conv(z_ref, k1, b1, r, base)
-        s1_ref[r, pl.ds(q * 4, 4)] = regroup((1.0 - act * act) * keep)
-        mid = (u_ref[r + 1, pl.ds(base, 128), :] + dot_split(act, p1[...])) * keep
-        m_ref[r, pl.ds(base, 128), :] = mid
-        z2_ref[r, pl.ds(base + 8, 128), :] = dot_split(mid, l2[...])
+        s1_ref[r, pl.ds(q * (size // 32), size // 32)] = regroup((1.0 - act * act) * keep)
+        mid = (u_ref[r + 1, pl.ds(base, size), :] + dot_split(act, p1[...], True)) * keep
+        m_ref[r, pl.ds(base, size), :] = mid
+        z2_ref[r, pl.ds(base + 8, size), :] = dot_split(mid, l2[...])
 
     @pl.loop(0, rows * pieces)
     def _(n):
         r, q = n // pieces, n % pieces
-        base = pl.multiple_of(q * 128, 128)
+        base = pl.multiple_of(q * size, size)
         act = conv(z2_ref, k2, b2, r, base)
-        s2_ref[r, pl.ds(q * 4, 4)] = regroup(1.0 - act * act)
-        out_ref[r, pl.ds(base, 128), :] = m_ref[r + 1, pl.ds(base, 128), :] + dot_split(act, p2[...])
+        s2_ref[r, pl.ds(q * (size // 32), size // 32)] = regroup(1.0 - act * act)
+        out_ref[r, pl.ds(base, size), :] = m_ref[r + 1, pl.ds(base, size), :] + dot_split(act, p2[...], True)
 
 
 def tangent_kernel(
-    rows, segs, low_ref, own_ref, high_ref, turned_ref, s1_ref, s2_ref, pd1, pd2, kern1, kern2, lift1, lift2,
-    sel_ref, rep_ref, maps_ref, x_ref, v_ref, t_ref, k1_ref, k2_ref,
+    rows, segs, low_ref, own_ref, high_ref, turned_ref, s1_ref, s2_ref, p1, p2, kern1, kern2, lift1, lift2,
+    sel_ref, rep_ref, spread_ref, maps_ref, x_ref, v_ref, t_ref, k1_ref, k2_ref, pd1, pd2,
 ):
     span = turned_ref.shape[2]
     tiles = span // 64
@@ -84,10 +93,14 @@
     x_ref[rows + 2 : rows + 4] = high_ref[...]
     v_ref[:, 0:8, :] = jnp.zeros((rows + 2, 8, segs * nm), F32)
     v_ref[:, span + 8 : span + 32, :] = jnp.zeros((rows + 2, 24, segs * nm), F32)
-    for kern, lift, k_ref in ((kern1, lift1, k1_ref), (kern2, lift2, k2_ref)):
-        wide = jnp.dot(lift[...].astype(F32), rep_ref[...], precision=HI, preferred_element_type=F32)
+    column = lax.broadcasted_iota(jnp.int32, (8, 256), 1) // 64
+    for kern, lift, proj, k_ref, pd in ((kern1, lift1, p1, k1_ref, pd1), (kern2, lift2, p2, k2_ref, pd2)):
+        wide = dot_turned(lift[...].astype(F32), rep_ref[...], 0, HI)
+        across = dot(proj[...], spread_ref[...])
+        for col in range(4):
+            pd[8 * col : 8 * col + 8, :] = jnp.where(column == col, across, 0.0)
         for col in range(8):
-            taps = jnp.dot(kern[...], sel_ref[col], precision=HI, preferred_element_type=F32)
+            taps = dot_turned(kern[...], sel_ref[col], 0, HI)
             k_ref[col // 4, (col % 4) * 64 : (col % 4 + 1) * 64, :] = (taps * wide).astype(BF16)
     maps_ref[...] = jnp.zeros_like(maps_ref)
 
@@ -96,7 +109,7 @@
         lhs = jnp.concatenate([(slopes[s : s + 1, :] * scale).astype(BF16) for s in range(segs)], axis=0)
         return dot(lhs, k_ref[h]).astype(BF16)
 
-    @pl.loop(0, (rows + 2) * tiles)
+    @pl.loop(0, (rows + 2) * tiles, unroll=2)
     def _(n):
         r, t = n // tiles, n % tiles
         at = pl.multiple_of(t * 64, 64)
@@ -111,7 +124,7 @@
 
     @pl.loop(0, rows)
     def _(r):
-        @pl.loop(0, tiles)
+        @pl.loop(0, tiles, unroll=2)
         def _(t):
             at = pl.multiple_of(t * 64, 64)
             bands = [band(s2_ref[r, 2 * t + h], pd2, k2_ref, h) for h in range(2)]
@@ -130,22 +143,100 @@
                 out = dot(both, near) + middle.astype(F32)[8:72]
                 t_ref[pl.ds(at, 64), lanes] = out.astype(BF16)
 
-        maps_ref[...] += dot(turned_ref[r], t_ref[...])
-
-
-def chain_kernel(segs, mats_ref, vecs_ref, start_ref, coeffs_ref, end_ref):
-    nm = mats_ref.shape[0]
-    current = start_ref[...]
-    for s in range(segs):
-        coeffs_ref[s : s + 1, :] = current[0:1, :]
-        current = (
-            lax.dot_general(
-                current, mats_ref[:, s * nm : (s + 1) * nm], (((1,), (1,)), ((), ())),
-                precision=HI, preferred_element_type=F32,
-            )
-            + vecs_ref[s : s + 1, :]
+        part = dot(turned_ref[r], t_ref[...])
+        for s in range(segs):
+            maps_ref[s * nm : (s + 1) * nm, :] += part[:, s * nm : (s + 1) * nm]
+
+
+def close_kernel(
+    segs, count, turns, mats_ref, vecs_ref, coeffs_ref, land_ref, sum_ref, all_ref, vland_ref, end_ref, start_ref,
+    send_m, recv_m, send_v, recv_v, send_a, recv_a, send_s, recv_s,
+):
+    nm = mats_ref.shape[1]
+    chunk = mats_ref.shape[0] // count
+    me, turn = lax.axis_index("space"), lax.axis_index("seg")
+    later, sooner = (turn + 1) % turns, (turn + turns - 1) % turns
+
+    def share(who):
+        return pl.ds(pl.multiple_of(who * chunk, 8), chunk)
+
+    barrier = pltpu.get_barrier_semaphore()
+    for d in range(1, count):
+        pl.semaphore_signal(barrier, inc=1, device_id={"space": (me + d) % count}, device_id_type=MESH)
+    if turns > 1:
+        pl.semaphore_signal(barrier, inc=1, device_id={"seg": sooner}, device_id_type=MESH)
+    pl.semaphore_wait(barrier, count - 1 + (turns > 1))
+
+    maps, vectors = [], []
+    for d in range(1, count):
+        target = (me + d) % count
+        copy = pltpu.make_async_remote_copy(
+            src_ref=mats_ref.at[share(target)], dst_ref=land_ref.at[d],
+            send_sem=send_m.at[d], recv_sem=recv_m.at[d],
+            device_id={"space": target}, device_id_type=MESH,
         )
-    end_ref[...] = current
+        copy.start()
+        maps.append(copy)
+    for d in range(1, count):
+        target = (me + d) % count
+        copy = pltpu.make_async_remote_copy(
+            src_ref=vecs_ref, dst_ref=vland_ref.at[d],
+            send_sem=send_v.at[d], recv_sem=recv_v.at[d],
+            device_id={"space": target}, device_id_type=MESH,
+        )
+        copy.start()
+        vectors.append(copy)
+    total = mats_ref[share(me), :]
+    for d in range(1, count):
+        maps[d - 1].wait_recv()
+        total = total + land_ref[d]
+    sum_ref[...] = total
+    gathers = []
+    for d in range(1, count):
+        copy = pltpu.make_async_remote_copy(
+            src_ref=sum_ref, dst_ref=all_ref.at[share(me)],
+            send_sem=send_a.at[d], recv_sem=recv_a.at[d],
+            device_id={"space": (me + d) % count}, device_id_type=MESH,
+        )
+        copy.start()
+        gathers.append(copy)
+    all_ref[share(me), :] = total
+    vland_ref[0] = vecs_ref[...]
+    for copy in vectors:
+        copy.wait_recv()
+    vecs = jnp.zeros((segs, nm), F32)
+    for who in range(count):
+        vecs = vecs + vland_ref[(me + count - who) % count]
+    for d in range(1, count):
+        source = (me + count - d) % count
+        pltpu.make_async_remote_copy(
+            src_ref=sum_ref, dst_ref=all_ref.at[share(source)],
+            send_sem=send_a.at[d], recv_sem=recv_a.at[d],
+            device_id={"space": (me + d) % count}, device_id_type=MESH,
+        ).wait_recv()
+
+    def chain(current, keep):
+        for s in range(segs):
+            if keep:
+                coeffs_ref[s : s + 1, :] = current[0:1, :]
+            if not keep or s < segs - 1:
+                current = dot_turned(current, all_ref[s * nm : (s + 1) * nm, :], 1, HI) + vecs[s : s + 1, :]
+        return current
+
+    current = jnp.zeros((8, nm), F32)
+    for step in range(turns - 1):
+        end_ref[step] = chain(current, False)
+        copy = pltpu.make_async_remote_copy(
+            src_ref=end_ref.at[step], dst_ref=start_ref.at[step],
+            send_sem=send_s.at[step], recv_sem=recv_s.at[step],
+            device_id={"seg": later}, device_id_type=MESH,
+        )
+        copy.start()
+        copy.wait()
+        current = jnp.where(turn == 0, 0.0, start_ref[step])
+    chain(current, True)
+    for copy in maps + vectors + gathers:
+        copy.wait_send()
 
 
 def selectors():
@@ -159,10 +250,11 @@
                 for col in range(8):
                     if 0 <= w - col < 3:
                         sel[col, 3 * i + w - col, lane] = 1.0
-    return sel, rep
+    return sel, rep, jnp.asarray(np.tile(np.eye(64, dtype=np.float32), (1, 4)), BF16)
 
 
 VM = pl.BlockSpec(memory_space=pltpu.VMEM)
+MESH = pl.DeviceIdType.MESH
 SM = pl.BlockSpec(memory_space=pltpu.SMEM)
 
 
@@ -211,22 +303,19 @@
         compiler_params=pltpu.CompilerParams(vmem_limit_bytes=56 * 2**20),
         cost_estimate=pl.CostEstimate(flops=10**8, bytes_accessed=10**7, transcendentals=10**6),
     )(
-        mask, u, lift_one.T, lift_two.T, proj_one.T, proj_two.T, kern_one.T, kern_two.T,
+        mask, u, lift_one.T, lift_two.T, proj_one, proj_two, kern_one.T, kern_two.T,
         bias_one[None], bias_two[None],
     )
     advanced = jnp.transpose(final.reshape(rows, cols, segs, fields), (2, 3, 0, 1))
     defects = (advanced - jnp.concatenate([states[1:], follow[None]], axis=0)).astype(BF16)
     vecs = jnp.einsum("sfrw,frwk->sk", defects, modes, preferred_element_type=F32)
 
-    sel, rep = selectors()
-    blockwise = np.kron(np.eye(4, dtype=np.float32), np.ones((fields, channels), np.float32))
-    pd1 = jnp.tile(proj_one.astype(F32), (4, 4)) * blockwise
-    pd2 = jnp.tile(proj_two.astype(F32), (4, 4)) * blockwise
+    sel, rep, spread = selectors()
     lines = cols * fields
     mats = pl.pallas_call(
         functools.partial(tangent_kernel, rows, segs),
-        out_shape=jax.ShapeDtypeStruct((nmodes, segs * nmodes), F32),
-        in_specs=[VM] * 14,
+        out_shape=jax.ShapeDtypeStruct((segs * nmodes, nmodes), F32),
+        in_specs=[VM] * 15,
         out_specs=VM,
         scratch_shapes=[
             pltpu.VMEM((rows + 4, lines + 32, nmodes), BF16),
@@ -234,28 +323,35 @@
             pltpu.VMEM((lines, segs * nmodes), BF16),
             pltpu.VMEM((2, 256, 256), BF16),
             pltpu.VMEM((2, 256, 256), BF16),
+            pltpu.VMEM((32, 256), F32),
+            pltpu.VMEM((32, 256), F32),
         ],
         compiler_params=pltpu.CompilerParams(vmem_limit_bytes=56 * 2**20),
         cost_estimate=pl.CostEstimate(flops=2 * 10**10, bytes_accessed=10**7, transcendentals=0),
     )(
-        low, own, high, turned, slope_one, slope_two, pd1, pd2, kern_one, kern_two, lift_one, lift_two, sel, rep
-    )
-
-    mats, vecs = lax.psum((mats, vecs), "space")
-    chain = pl.pallas_call(
-        functools.partial(chain_kernel, segs),
-        out_shape=(
-            jax.ShapeDtypeStruct((segs, nmodes), F32),
-            jax.ShapeDtypeStruct((8, nmodes), F32),
-        ),
-        in_specs=[VM] * 3,
-        out_specs=(VM, VM),
-    )
-    start = jnp.zeros((8, nmodes), F32)
-    for _ in range(turns - 1):
-        end = chain(mats, vecs, start)[1]
-        start = lax.ppermute(end, "seg", [(i, i + 1) for i in range(turns - 1)])
-    coeffs = chain(mats, vecs, start)[0]
+        low, own, high, turned, slope_one, slope_two, proj_one, proj_two, kern_one.T, kern_two.T,
+        lift_one.T, lift_two.T, sel, rep, spread,
+    )
+
+    chunk = segs * nmodes // count
+    dma = pltpu.SemaphoreType.DMA
+    coeffs = pl.pallas_call(
+        functools.partial(close_kernel, segs, count, turns),
+        out_shape=jax.ShapeDtypeStruct((segs, nmodes), F32),
+        in_specs=[VM] * 2,
+        out_specs=VM,
+        scratch_shapes=[
+            pltpu.VMEM((count, chunk, nmodes), F32),
+            pltpu.VMEM((chunk, nmodes), F32),
+            pltpu.VMEM((segs * nmodes, nmodes), F32),
+            pltpu.VMEM((count, segs, nmodes), F32),
+            pltpu.VMEM((turns, 8, nmodes), F32),
+            pltpu.VMEM((turns, 8, nmodes), F32),
+            dma((count,)), dma((count,)), dma((count,)), dma((count,)), dma((count,)), dma((count,)),
+            dma((turns,)), dma((turns,)),
+        ],
+        compiler_params=pltpu.CompilerParams(collective_id=0, has_side_effects=True),
+    )(mats, vecs)
     return advanced, coeffs
 
 

time: 246 us -> 144 us (0.59); the launches traced: 243 us -> 144 us
  waiting for transfers between devices: 67.7 us -> 0.01 us
  blocking collectives: 14.2 us -> 0 us
  between operations: 14.2 us -> 0.74 us
  Pallas kernels: 118 us -> 115 us
    psum x1 -> x0, waiting for transfers between devices: 52.9 us -> none  [on_device(): mats, vecs = lax.psum((mats, vecs), 'space')]
    pallas_call x2 -> x1, Pallas kernels: 7.92 us -> 37 us  [on_device(): pl.pallas_call(functools.partial(close_kernel, segs, count, turns), out_s...]
    pallas_call x1, Pallas kernels: 80.8 us -> 58.3 us  [on_device(): pl.pallas_call(functools.partial(tangent_kernel, rows, segs), out_shape=j...]
    psum x1 -> x0, blocking collectives: 14.2 us -> none  [on_device(): mats, vecs = lax.psum((mats, vecs), 'space')]
    ppermute x1, waiting for transfers between devices: 11.1 us -> 0.01 us  [on_device(): after = lax.ppermute(states[:, :, :2], 'space', up)]
    pallas_call x1, Pallas kernels: 28.9 us -> 20 us  [on_device(): pl.pallas_call(functools.partial(advance_kernel, rows), out_shape=(jax.Sh...]
    ppermute x1 -> x0, waiting for transfers between devices: 3.5 us -> none  [on_device(): start = lax.ppermute(end, 'seg', [(i, i + 1) for i in range(turns - 1)])]
    unnamed x31 -> x10, local copies, waits for them, and re-layouts: 6.69 us -> 3.98 us
  transfers between devices with their start and end apart: 7 -> 5, of which waited for: 4 -> 0; matrix products, arithmetic and copies ran while one was open for 5% -> 8% of each run, Pallas kernels for 12% -> 14%
where the time goes in v2:
time: 144 us
  Pallas kernels  115 us (80%)
  starting transfers between devices  13.6 us (9%)
  local copies, waits for them, and re-layouts  12.9 us (9%)
    pallas_call x1, Pallas kernels, on_device(): pl.pallas_call(functools.partial(tangent_kernel, rows, segs), out_shape=j...  58.3 us
    pallas_call x1, Pallas kernels, on_device(): pl.pallas_call(functools.partial(close_kernel, segs, count, turns), out_s...  37 us
    pallas_call x1, Pallas kernels, on_device(): pl.pallas_call(functools.partial(advance_kernel, rows), out_shape=(jax.Sh...  20 us
    ppermute x1, starting transfers between devices, on_device(): high = lax.ppermute(own[:2], 'space', up)  5.42 us
    unnamed x10, local copies, waits for them, and re-layouts  3.98 us
    ppermute x1, starting transfers between devices, on_device(): lax.ppermute(states[0], 'seg', [(i + 1, i) for i in range(turns - 1)])  3.41 us
    transpose x1, local copies, waits for them, and re-layouts, on_device(): jnp.transpose(extended, (2, 3, 0, 1)).reshape(rows + 4, cols * segs, fields)  3.11 us
  transfers between devices with their start and end apart: 5, of which 0 were waited for; matrix products, arithmetic and copies ran while one was open for 8% of the time, Pallas kernels for 14%

profile of v2, /device:TPU:31, one launch (start us, length us, event | category | flops | bytes accessed | tf_op | source)
XLA Modules:
  0.0 144.1 jit_solution(8986615088742264415)
XLA Ops:
  0.6 1.0 fusion.2
  1.7 2.2 %collective-permute-start.1 = (f32[8,8,2,128]{3,2,1,0:T(2,128)S(1)}, f32[8,8,2,128]{3,2,1,0:T(2,128)S(1)}, u32[]{:S(2)}, u32[]{:S(2)}) collective-permute-start(f32[8,8,2,128]{3,2,1,0:T(2,128)S(1)} %get-tuple-element.11), channel_id=1, source_target_pairs={{2,0},{4,2},{6,4},{8,6},{10,8},{12,10},{14,12},{3,1},{5,3},{7,5},{... | collective-permute-start | bytes 196616 | tf_op jit(solution)/shard_map/ppermute | solution.py:272
  3.8 1.3 collective-permute-start
  5.1 1.9 %copy.31 = bf16[8,4,128,128]{3,0,2,1:T(8,128)(2,1)S(1)} copy(bf16[8,4,128,128]{3,2,1,0:T(8,128)(2,1)} %param.13) | data formatting | bytes 2097152 | tf_op args[0]
  7.1 0.0 copy-start.1
  7.1 0.1 pad_slice_fusion
  7.2 1.3 collective-permute-start.2
  8.4 5.4 %collective-permute-start.3 = (bf16[2,1056,128]{2,1,0:T(8,128)(2,1)S(1)}, bf16[2,1056,128]{2,1,0:T(8,128)(2,1)}, u32[]{:S(2)}, u32[]{:S(2)}) collective-permute-start(bf16[2,1056,128]{2,1,0:T(8,128)(2,1)S(1)} %get-tuple-element.8), channel_id=1, source_target_pairs={{2,0},{4,2},{6,4},{8,6},{10,8},{12,10},{14,12},{3,1},{5,3},{7,5},{... | collective-permute-start | bytes 1622024 | tf_op jit(solution)/shard_map/ppermute | solution.py:280
  13.9 0.0 copy-done.1
  13.9 3.4 %collective-permute-start.4 = (f32[8,4,128]{2,1,0:T(4,128)S(1)}, f32[8,4,128]{2,1,0:T(4,128)S(1)}, u32[]{:S(2)}, u32[]{:S(2)}) collective-permute-start(f32[8,4,128]{2,1,0:T(4,128)S(1)} %slice_bitcast_fusion), channel_id=1, source_target_pairs={{1,0},{3,2},{5,4},{7,6},{9,8},{11,10},{13,12},{15,14},{17,16},{19,... | collective-permute-start | bytes 49160 | tf_op jit(solution)/shard_map/ppermute | solution.py:274
  17.3 0.5 and_convert_fusion.mask_ref
  17.8 1.3 copy.25
  19.1 1.1 pad.4.own_ref
  20.3 0.0 collective-permute-done.1
  20.3 0.0 collective-permute-done
  20.3 0.1 maximum_bitcast_fusion
  20.4 3.1 %copy.22 = f32[8,128,8,8]{3,2,1,0:T(8,128)} copy(f32[8,128,8,8]{1,0,3,2:T(8,128)S(1)} %maximum_bitcast_fusion) | data formatting | bytes 524288 | tf_op jit(solution)/shard_map/transpose | solution.py:283
  23.5 20.0 %shard_map.140 = (f32[6,32,8,256]{3,2,1,0:T(8,128)}, f32[4,32,8,256]{3,2,1,0:T(8,128)}, f32[4,1024,8]{2,1,0:T(8,128)}) custom-call(f32[6]{0:T(128)} %and_convert_fusion.mask_ref, f32[8,1024,8]{2,1,0:T(8,128)} %bitcast.29, bf16[8,64]{1,0:T(8,128)(2,1)} %bitcast.38, bf16[8,64]{1,0:T(8,128)(2,1)} %bitcast.40, bf16[8,64]{1,0:T(8,128)(2,1)} %p1.3, ...), custom_call_target="tpu_custom_call" | custom-call | flops 100000000 | bytes 10000000 | tf_op jit(solution)/shard_map/pallas_call | solution.py:289
  43.5 0.0 slice-start
  43.5 0.0 copy-start
  43.5 2.3 %copy.23 = f32[4,128,8,8]{1,0,3,2:T(4,128)S(1)} copy(f32[4,128,8,8]{3,2,1,0:T(8,128)} %bitcast.30) | data formatting | bytes 262144 | tf_op jit(solution)/shard_map/reshape | solution.py:309
  45.8 0.0 copy-start.2
  45.8 0.0 collective-permute-done.4
  45.8 0.0 slice-done
  45.9 0.0 copy-done
  45.9 0.9 convolution_bitcast_fusion.vecs_ref
  46.7 0.0 collective-permute-done.2.low_ref
  46.8 0.0 copy-start.3
  46.8 0.0 collective-permute-done.3.high_ref
  46.8 0.8 copy-done.3
  47.5 58.3 %shard_map.141.mats_ref = f32[1024,128]{1,0:T(8,128)} custom-call(bf16[2,1056,128]{2,1,0:T(8,128)(2,1)} %copy-done.3, bf16[4,1056,128]{2,1,0:T(8,128)(2,1)} %pad.4.own_ref, bf16[2,1056,128]{2,1,0:T(8,128)(2,1)} %collective-permute-done.3.high_ref, bf16[4,128,1024]{2,1,0:T(8,128)(2,1)} %bitcast.31, f32[6,32,8,256]{3,2,1,0:T(8,128)} %get-tuple-element.6.s1_ref, ...), custom_call_target="tpu_custom_call" | custom-call | flops 20000000000 | bytes 10000000 | tf_op jit(solution)/shard_map/pallas_call | solution.py:315
  105.9 0.0 copy-done.2
  105.9 37.0 %shard_map.142 = f32[8,128]{1,0:T(8,128)} custom-call(f32[1024,128]{1,0:T(8,128)} %shard_map.141.mats_ref, f32[8,128]{1,0:T(8,128)} %convolution_bitcast_fusion.vecs_ref), custom_call_target="tpu_custom_call" | custom-call | tf_op jit(solution)/shard_map/pallas_call | solution.py:338
  142.9 1.3 copy.33
  (2 shorter events, 0.0 us)
Async XLA Ops:
  1.7 18.6 %collective-permute-start.1 = (f32[8,8,2,128]{3,2,1,0:T(2,128)S(1)}, f32[8,8,2,128]{3,2,1,0:T(2,128)S(1)}, u32[]{:S(2)}, u32[]{:S(2)}) collective-permute-start(f32[8,8,2,128]{3,2,1,0:T(2,128)S(1)} %get-tuple-element.11), channel_id=1, source_target_pairs={{2,0},{4,2},{6,4},{8,6},{10,8},{12,10},{14,12},{3,1},{5,3},{7,5},{... | collective-permute-start | bytes 196616 | tf_op jit(solution)/shard_map/ppermute | solution.py:272
  3.8 16.4 %collective-permute-start = (f32[8,8,2,128]{3,2,1,0:T(2,128)S(1)}, f32[8,8,2,128]{3,2,1,0:T(2,128)S(1)}, u32[]{:S(2)}, u32[]{:S(2)}) collective-permute-start(f32[8,8,2,128]{3,2,1,0:T(2,128)S(1)} %get-tuple-element.10), channel_id=1, source_target_pairs={{0,2},{2,4},{4,6},{6,8},{8,10},{10,12},{12,14},{1,3},{3,5},{5,7},{... | collective-permute-start | bytes 196616 | tf_op jit(solution)/shard_map/ppermute | solution.py:271
  7.1 6.8 %copy-start.1 = (f32[8,8,4,128]{3,2,1,0:T(4,128)S(1)}, f32[8,8,4,128]{3,2,1,0:T(4,128)}, u32[]{:S(2)}) copy-start(f32[8,8,4,128]{3,2,1,0:T(4,128)} %param.14) | copy-start | bytes 393220
  7.2 39.6 %collective-permute-start.2 = (bf16[2,1056,128]{2,1,0:T(8,128)(2,1)S(1)}, bf16[2,1056,128]{2,1,0:T(8,128)(2,1)S(1)}, u32[]{:S(2)}, u32[]{:S(2)}) collective-permute-start(bf16[2,1056,128]{2,1,0:T(8,128)(2,1)S(1)} %get-tuple-element.9), channel_id=1, source_target_pairs={{0,2},{2,4},{4,6},{6,8},{8,10},{10,12},{12,14},{1,3},{3,5},{5,7},{... | collective-permute-start | bytes 1622024 | tf_op jit(solution)/shard_map/ppermute | solution.py:279
  8.4 38.3 %collective-permute-start.3 = (bf16[2,1056,128]{2,1,0:T(8,128)(2,1)S(1)}, bf16[2,1056,128]{2,1,0:T(8,128)(2,1)}, u32[]{:S(2)}, u32[]{:S(2)}) collective-permute-start(bf16[2,1056,128]{2,1,0:T(8,128)(2,1)S(1)} %get-tuple-element.8), channel_id=1, source_target_pairs={{2,0},{4,2},{6,4},{8,6},{10,8},{12,10},{14,12},{3,1},{5,3},{7,5},{... | collective-permute-start | bytes 1622024 | tf_op jit(solution)/shard_map/ppermute | solution.py:280
  13.9 31.9 %collective-permute-start.4 = (f32[8,4,128]{2,1,0:T(4,128)S(1)}, f32[8,4,128]{2,1,0:T(4,128)S(1)}, u32[]{:S(2)}, u32[]{:S(2)}) collective-permute-start(f32[8,4,128]{2,1,0:T(4,128)S(1)} %slice_bitcast_fusion), channel_id=1, source_target_pairs={{1,0},{3,2},{5,4},{7,6},{9,8},{11,10},{13,12},{15,14},{17,16},{19,... | collective-permute-start | bytes 49160 | tf_op jit(solution)/shard_map/ppermute | solution.py:274
  43.5 2.3 %slice-start = ((f32[8,8,4,128]{3,2,1,0:T(4,128)}), f32[7,8,4,128]{3,2,1,0:T(4,128)S(1)}, s32[]{:S(2)}) async-start(f32[8,8,4,128]{3,2,1,0:T(4,128)} %param.14), calls=%async_computation | async-start | bytes 229376 | tf_op jit(solution)/shard_map/slice | solution.py:310
  43.5 2.3 %copy-start = (bf16[8,4,128,128]{3,2,1,0:T(8,128)(2,1)S(1)}, bf16[8,4,128,128]{3,2,1,0:T(8,128)(2,1)}, u32[]{:S(2)}) copy-start(bf16[8,4,128,128]{3,2,1,0:T(8,128)(2,1)} %param.13) | copy-start | bytes 3145732
  45.8 60.1 %copy-start.2 = (f32[4,128,8,8]{1,0,3,2:T(4,128)}, f32[4,128,8,8]{1,0,3,2:T(4,128)S(1)}, u32[]{:S(2)}) copy-start(f32[4,128,8,8]{1,0,3,2:T(4,128)S(1)} %copy.23) | copy-start | bytes 393220
  46.8 0.8 copy-start.3

commit v3 on v2

--- a/solution.py
+++ b/solution.py
@@ -47,7 +47,7 @@
     z2_ref[:, 0:8, :] = edge2
     z2_ref[:, span + 8 : span + 16, :] = edge2
 
-    @pl.loop(0, rows + 4)
+    @pl.loop(0, rows + 4, unroll=2)
     def _(r):
         z_ref[r, 8 : span + 8, :] = dot_split(u_ref[r], l1[...])
 
@@ -61,7 +61,7 @@
                 acc = acc + taps[3 * i + j : 3 * i + j + 1, :] * ref[r + i, pl.ds(base + 8 * j, size), :]
         return jnp.tanh(acc)
 
-    @pl.loop(0, (rows + 2) * pieces)
+    @pl.loop(0, (rows + 2) * pieces, unroll=2)
     def _(n):
         r, q = n // pieces, n % pieces
         base = pl.multiple_of(q * size, size)
@@ -72,7 +72,7 @@
         m_ref[r, pl.ds(base, size), :] = mid
         z2_ref[r, pl.ds(base + 8, size), :] = dot_split(mid, l2[...])
 
-    @pl.loop(0, rows * pieces)
+    @pl.loop(0, rows * pieces, unroll=2)
     def _(n):
         r, q = n // pieces, n % pieces
         base = pl.multiple_of(q * size, size)
@@ -109,7 +109,7 @@
         lhs = jnp.concatenate([(slopes[s : s + 1, :] * scale).astype(BF16) for s in range(segs)], axis=0)
         return dot(lhs, k_ref[h]).astype(BF16)
 
-    @pl.loop(0, (rows + 2) * tiles, unroll=2)
+    @pl.loop(0, (rows + 2) * tiles, unroll=4)
     def _(n):
         r, t = n // tiles, n % tiles
         at = pl.multiple_of(t * 64, 64)
@@ -124,7 +124,7 @@
 
     @pl.loop(0, rows)
     def _(r):
-        @pl.loop(0, tiles, unroll=2)
+        @pl.loop(0, tiles, unroll=4)
         def _(t):
             at = pl.multiple_of(t * 64, 64)
             bands = [band(s2_ref[r, 2 * t + h], pd2, k2_ref, h) for h in range(2)]

time: 144 us -> 130 us (0.903)
  Pallas kernels: 115 us -> 101 us
    pallas_call x1, Pallas kernels: 58.3 us -> 46.9 us  [on_device(): pl.pallas_call(functools.partial(tangent_kernel, rows, segs), out_shape=j...]
    pallas_call x1, Pallas kernels: 20 us -> 16.6 us  [on_device(): pl.pallas_call(functools.partial(advance_kernel, rows), out_shape=(jax.Sh...]
  transfers between devices with their start and end apart: 5 -> 5, of which waited for: 0 -> 0; matrix products, arithmetic and copies ran while one was open for 8% -> 9% of each run, Pallas kernels for 14% -> 13%
where the time goes in v3:
time: 130 us; the launch traced here: 129 us
  Pallas kernels  101 us (78%)
  starting transfers between devices  13.6 us (10%)
  local copies, waits for them, and re-layouts  12.9 us (10%)
    pallas_call x1, Pallas kernels, on_device(): pl.pallas_call(functools.partial(tangent_kernel, rows, segs), out_shape=j...  46.9 us
    pallas_call x1, Pallas kernels, on_device(): pl.pallas_call(functools.partial(close_kernel, segs, count, turns), out_s...  37 us
    pallas_call x1, Pallas kernels, on_device(): pl.pallas_call(functools.partial(advance_kernel, rows), out_shape=(jax.Sh...  16.6 us
    ppermute x1, starting transfers between devices, on_device(): high = lax.ppermute(own[:2], 'space', up)  5.42 us
    unnamed x10, local copies, waits for them, and re-layouts  3.98 us
    ppermute x1, starting transfers between devices, on_device(): lax.ppermute(states[0], 'seg', [(i + 1, i) for i in range(turns - 1)])  3.41 us
    transpose x1, local copies, waits for them, and re-layouts, on_device(): jnp.transpose(extended, (2, 3, 0, 1)).reshape(rows + 4, cols * segs, fields)  3.11 us
  transfers between devices with their start and end apart: 5, of which 0 were waited for; matrix products, arithmetic and copies ran while one was open for 9% of the time, Pallas kernels for 13%

profile of v3, /device:TPU:31, one launch (start us, length us, event | category | flops | bytes accessed | tf_op | source)
XLA Modules:
  0.0 129.4 jit_solution(4035705056388249074)
XLA Ops:
  0.6 1.0 fusion.2
  1.7 2.2 %collective-permute-start.1 = (f32[8,8,2,128]{3,2,1,0:T(2,128)S(1)}, f32[8,8,2,128]{3,2,1,0:T(2,128)S(1)}, u32[]{:S(2)}, u32[]{:S(2)}) collective-permute-start(f32[8,8,2,128]{3,2,1,0:T(2,128)S(1)} %get-tuple-element.11), channel_id=1, source_target_pairs={{2,0},{4,2},{6,4},{8,6},{10,8},{12,10},{14,12},{3,1},{5,3},{7,5},{... | collective-permute-start | bytes 196616 | tf_op jit(solution)/shard_map/ppermute | solution.py:272
  3.8 1.3 collective-permute-start
  5.1 1.9 %copy.31 = bf16[8,4,128,128]{3,0,2,1:T(8,128)(2,1)S(1)} copy(bf16[8,4,128,128]{3,2,1,0:T(8,128)(2,1)} %param.13) | data formatting | bytes 2097152 | tf_op args[0]
  7.1 0.0 copy-start.1
  7.1 0.1 pad_slice_fusion
  7.2 1.3 collective-permute-start.2
  8.4 5.4 %collective-permute-start.3 = (bf16[2,1056,128]{2,1,0:T(8,128)(2,1)S(1)}, bf16[2,1056,128]{2,1,0:T(8,128)(2,1)}, u32[]{:S(2)}, u32[]{:S(2)}) collective-permute-start(bf16[2,1056,128]{2,1,0:T(8,128)(2,1)S(1)} %get-tuple-element.8), channel_id=1, source_target_pairs={{2,0},{4,2},{6,4},{8,6},{10,8},{12,10},{14,12},{3,1},{5,3},{7,5},{... | collective-permute-start | bytes 1622024 | tf_op jit(solution)/shard_map/ppermute | solution.py:280
  13.9 0.0 copy-done.1
  13.9 3.4 %collective-permute-start.4 = (f32[8,4,128]{2,1,0:T(4,128)S(1)}, f32[8,4,128]{2,1,0:T(4,128)S(1)}, u32[]{:S(2)}, u32[]{:S(2)}) collective-permute-start(f32[8,4,128]{2,1,0:T(4,128)S(1)} %slice_bitcast_fusion), channel_id=1, source_target_pairs={{1,0},{3,2},{5,4},{7,6},{9,8},{11,10},{13,12},{15,14},{17,16},{19,... | collective-permute-start | bytes 49160 | tf_op jit(solution)/shard_map/ppermute | solution.py:274
  17.3 0.5 and_convert_fusion.mask_ref
  17.8 1.3 %copy.25 = bf16[4,1024,128]{1,2,0:T(8,128)(2,1)} copy(bf16[4,1024,128]{2,1,0:T(8,128)(2,1)S(1)} %bitcast.27) | data formatting | bytes 2097152 | tf_op jit(solution)/shard_map/reshape | solution.py:276
  19.1 1.1 pad.4.own_ref
  20.3 0.0 collective-permute-done.1
  20.3 0.0 collective-permute-done
  20.3 0.1 maximum_bitcast_fusion
  20.4 3.1 %copy.22 = f32[8,128,8,8]{3,2,1,0:T(8,128)} copy(f32[8,128,8,8]{1,0,3,2:T(8,128)S(1)} %maximum_bitcast_fusion) | data formatting | bytes 524288 | tf_op jit(solution)/shard_map/transpose | solution.py:283
  23.5 16.6 %shard_map.140 = (f32[6,32,8,256]{3,2,1,0:T(8,128)}, f32[4,32,8,256]{3,2,1,0:T(8,128)}, f32[4,1024,8]{2,1,0:T(8,128)}) custom-call(f32[6]{0:T(128)} %and_convert_fusion.mask_ref, f32[8,1024,8]{2,1,0:T(8,128)} %bitcast.29, bf16[8,64]{1,0:T(8,128)(2,1)} %bitcast.38, bf16[8,64]{1,0:T(8,128)(2,1)} %bitcast.40, bf16[8,64]{1,0:T(8,128)(2,1)} %p1.3, ...), custom_call_target="tpu_custom_call" | custom-call | flops 100000000 | bytes 10000000 | tf_op jit(solution)/shard_map/pallas_call | solution.py:289
  40.1 0.0 slice-start
  40.1 0.0 copy-start
  40.1 2.3 %copy.23 = f32[4,128,8,8]{1,0,3,2:T(4,128)S(1)} copy(f32[4,128,8,8]{3,2,1,0:T(8,128)} %bitcast.30) | data formatting | bytes 262144 | tf_op jit(solution)/shard_map/reshape | solution.py:309
  42.4 0.0 copy-start.2
  42.4 0.0 collective-permute-done.4
  42.4 0.0 slice-done
  42.5 0.0 copy-done
  42.5 0.9 convolution_bitcast_fusion.vecs_ref
  43.3 0.0 collective-permute-done.2.low_ref
  43.4 0.0 copy-start.3
  43.4 0.0 collective-permute-done.3.high_ref
  43.4 0.8 copy-done.3
  44.1 46.9 %shard_map.141.mats_ref = f32[1024,128]{1,0:T(8,128)} custom-call(bf16[2,1056,128]{2,1,0:T(8,128)(2,1)} %copy-done.3, bf16[4,1056,128]{2,1,0:T(8,128)(2,1)} %pad.4.own_ref, bf16[2,1056,128]{2,1,0:T(8,128)(2,1)} %collective-permute-done.3.high_ref, bf16[4,128,1024]{2,1,0:T(8,128)(2,1)} %bitcast.31, f32[6,32,8,256]{3,2,1,0:T(8,128)} %get-tuple-element.6.s1_ref, ...), custom_call_target="tpu_custom_call" | custom-call | flops 20000000000 | bytes 10000000 | tf_op jit(solution)/shard_map/pallas_call | solution.py:315
  91.1 0.0 copy-done.2
  91.1 37.0 %shard_map.142 = f32[8,128]{1,0:T(8,128)} custom-call(f32[1024,128]{1,0:T(8,128)} %shard_map.141.mats_ref, f32[8,128]{1,0:T(8,128)} %convolution_bitcast_fusion.vecs_ref), custom_call_target="tpu_custom_call" | custom-call | tf_op jit(solution)/shard_map/pallas_call | solution.py:338
  128.1 1.3 copy.33
  (2 shorter events, 0.0 us)
Async XLA Ops:
  1.7 18.6 %collective-permute-start.1 = (f32[8,8,2,128]{3,2,1,0:T(2,128)S(1)}, f32[8,8,2,128]{3,2,1,0:T(2,128)S(1)}, u32[]{:S(2)}, u32[]{:S(2)}) collective-permute-start(f32[8,8,2,128]{3,2,1,0:T(2,128)S(1)} %get-tuple-element.11), channel_id=1, source_target_pairs={{2,0},{4,2},{6,4},{8,6},{10,8},{12,10},{14,12},{3,1},{5,3},{7,5},{... | collective-permute-start | bytes 196616 | tf_op jit(solution)/shard_map/ppermute | solution.py:272
  3.8 16.4 %collective-permute-start = (f32[8,8,2,128]{3,2,1,0:T(2,128)S(1)}, f32[8,8,2,128]{3,2,1,0:T(2,128)S(1)}, u32[]{:S(2)}, u32[]{:S(2)}) collective-permute-start(f32[8,8,2,128]{3,2,1,0:T(2,128)S(1)} %get-tuple-element.10), channel_id=1, source_target_pairs={{0,2},{2,4},{4,6},{6,8},{8,10},{10,12},{12,14},{1,3},{3,5},{5,7},{... | collective-permute-start | bytes 196616 | tf_op jit(solution)/shard_map/ppermute | solution.py:271
  7.1 6.8 %copy-start.1 = (f32[8,8,4,128]{3,2,1,0:T(4,128)S(1)}, f32[8,8,4,128]{3,2,1,0:T(4,128)}, u32[]{:S(2)}) copy-start(f32[8,8,4,128]{3,2,1,0:T(4,128)} %param.14) | copy-start | bytes 393220
  7.2 36.2 %collective-permute-start.2 = (bf16[2,1056,128]{2,1,0:T(8,128)(2,1)S(1)}, bf16[2,1056,128]{2,1,0:T(8,128)(2,1)S(1)}, u32[]{:S(2)}, u32[]{:S(2)}) collective-permute-start(bf16[2,1056,128]{2,1,0:T(8,128)(2,1)S(1)} %get-tuple-element.9), channel_id=1, source_target_pairs={{0,2},{2,4},{4,6},{6,8},{8,10},{10,12},{12,14},{1,3},{3,5},{5,7},{... | collective-permute-start | bytes 1622024 | tf_op jit(solution)/shard_map/ppermute | solution.py:279
  8.4 34.9 %collective-permute-start.3 = (bf16[2,1056,128]{2,1,0:T(8,128)(2,1)S(1)}, bf16[2,1056,128]{2,1,0:T(8,128)(2,1)}, u32[]{:S(2)}, u32[]{:S(2)}) collective-permute-start(bf16[2,1056,128]{2,1,0:T(8,128)(2,1)S(1)} %get-tuple-element.8), channel_id=1, source_target_pairs={{2,0},{4,2},{6,4},{8,6},{10,8},{12,10},{14,12},{3,1},{5,3},{7,5},{... | collective-permute-start | bytes 1622024 | tf_op jit(solution)/shard_map/ppermute | solution.py:280
  13.9 28.5 %collective-permute-start.4 = (f32[8,4,128]{2,1,0:T(4,128)S(1)}, f32[8,4,128]{2,1,0:T(4,128)S(1)}, u32[]{:S(2)}, u32[]{:S(2)}) collective-permute-start(f32[8,4,128]{2,1,0:T(4,128)S(1)} %slice_bitcast_fusion), channel_id=1, source_target_pairs={{1,0},{3,2},{5,4},{7,6},{9,8},{11,10},{13,12},{15,14},{17,16},{19,... | collective-permute-start | bytes 49160 | tf_op jit(solution)/shard_map/ppermute | solution.py:274
  40.1 2.3 %slice-start = ((f32[8,8,4,128]{3,2,1,0:T(4,128)}), f32[7,8,4,128]{3,2,1,0:T(4,128)S(1)}, s32[]{:S(2)}) async-start(f32[8,8,4,128]{3,2,1,0:T(4,128)} %param.14), calls=%async_computation | async-start | bytes 229376 | tf_op jit(solution)/shard_map/slice | solution.py:310
  40.1 2.3 %copy-start = (bf16[8,4,128,128]{3,2,1,0:T(8,128)(2,1)S(1)}, bf16[8,4,128,128]{3,2,1,0:T(8,128)(2,1)}, u32[]{:S(2)}) copy-start(bf16[8,4,128,128]{3,2,1,0:T(8,128)(2,1)} %param.13) | copy-start | bytes 3145732
  42.4 48.7 %copy-start.2 = (f32[4,128,8,8]{1,0,3,2:T(4,128)}, f32[4,128,8,8]{1,0,3,2:T(4,128)S(1)}, u32[]{:S(2)}) copy-start(f32[4,128,8,8]{1,0,3,2:T(4,128)S(1)} %copy.23) | copy-start | bytes 393220
  43.4 0.8 copy-start.3

commit v4 on v3

--- a/solution.py
+++ b/solution.py
@@ -47,7 +47,7 @@
     z2_ref[:, 0:8, :] = edge2
     z2_ref[:, span + 8 : span + 16, :] = edge2
 
-    @pl.loop(0, rows + 4, unroll=2)
+    @pl.loop(0, rows + 4, unroll=4)
     def _(r):
         z_ref[r, 8 : span + 8, :] = dot_split(u_ref[r], l1[...])
 
@@ -61,7 +61,7 @@
                 acc = acc + taps[3 * i + j : 3 * i + j + 1, :] * ref[r + i, pl.ds(base + 8 * j, size), :]
         return jnp.tanh(acc)
 
-    @pl.loop(0, (rows + 2) * pieces, unroll=2)
+    @pl.loop(0, (rows + 2) * pieces, unroll=4)
     def _(n):
         r, q = n // pieces, n % pieces
         base = pl.multiple_of(q * size, size)
@@ -72,7 +72,7 @@
         m_ref[r, pl.ds(base, size), :] = mid
         z2_ref[r, pl.ds(base + 8, size), :] = dot_split(mid, l2[...])
 
-    @pl.loop(0, rows * pieces, unroll=2)
+    @pl.loop(0, rows * pieces, unroll=4)
     def _(n):
         r, q = n // pieces, n % pieces
         base = pl.multiple_of(q * size, size)
@@ -109,7 +109,7 @@
         lhs = jnp.concatenate([(slopes[s : s + 1, :] * scale).astype(BF16) for s in range(segs)], axis=0)
         return dot(lhs, k_ref[h]).astype(BF16)
 
-    @pl.loop(0, (rows + 2) * tiles, unroll=4)
+    @pl.loop(0, (rows + 2) * tiles, unroll=8)
     def _(n):
         r, t = n // tiles, n % tiles
         at = pl.multiple_of(t * 64, 64)
@@ -124,7 +124,7 @@
 
     @pl.loop(0, rows)
     def _(r):
-        @pl.loop(0, tiles, unroll=4)
+        @pl.loop(0, tiles, unroll=8)
         def _(t):
             at = pl.multiple_of(t * 64, 64)
             bands = [band(s2_ref[r, 2 * t + h], pd2, k2_ref, h) for h in range(2)]

time: 130 us -> 120 us (0.923)
  Pallas kernels: 101 us -> 91.3 us
    pallas_call x1, Pallas kernels: 46.9 us -> 41.3 us  [on_device(): pl.pallas_call(functools.partial(tangent_kernel, rows, segs), out_shape=j...]
    pallas_call x1, Pallas kernels: 16.6 us -> 13.1 us  [on_device(): pl.pallas_call(functools.partial(advance_kernel, rows), out_shape=(jax.Sh...]
  transfers between devices with their start and end apart: 5 -> 5, of which waited for: 0 -> 0; matrix products, arithmetic and copies ran while one was open for 9% -> 9% of each run, Pallas kernels for 13% -> 11%
where the time goes in v4:
time: 120 us
  Pallas kernels  91.3 us (76%)
  starting transfers between devices  13.6 us (11%)
  local copies, waits for them, and re-layouts  12.9 us (11%)
    pallas_call x1, Pallas kernels, on_device(): pl.pallas_call(functools.partial(tangent_kernel, rows, segs), out_shape=j...  41.3 us
    pallas_call x1, Pallas kernels, on_device(): pl.pallas_call(functools.partial(close_kernel, segs, count, turns), out_s...  37 us
    pallas_call x1, Pallas kernels, on_device(): pl.pallas_call(functools.partial(advance_kernel, rows), out_shape=(jax.Sh...  13.1 us
    ppermute x1, starting transfers between devices, on_device(): high = lax.ppermute(own[:2], 'space', up)  5.42 us
    unnamed x10, local copies, waits for them, and re-layouts  3.98 us
    ppermute x1, starting transfers between devices, on_device(): lax.ppermute(states[0], 'seg', [(i + 1, i) for i in range(turns - 1)])  3.41 us
    transpose x1, local copies, waits for them, and re-layouts, on_device(): jnp.transpose(extended, (2, 3, 0, 1)).reshape(rows + 4, cols * segs, fields)  3.11 us
  transfers between devices with their start and end apart: 5, of which 0 were waited for; matrix products, arithmetic and copies ran while one was open for 9% of the time, Pallas kernels for 11%

profile of v4, /device:TPU:31, one launch (start us, length us, event | category | flops | bytes accessed | tf_op | source)
XLA Modules:
  0.0 120.1 jit_solution(8683800289338131377)
XLA Ops:
  0.6 1.0 fusion.2
  1.7 2.2 %collective-permute-start.1 = (f32[8,8,2,128]{3,2,1,0:T(2,128)S(1)}, f32[8,8,2,128]{3,2,1,0:T(2,128)S(1)}, u32[]{:S(2)}, u32[]{:S(2)}) collective-permute-start(f32[8,8,2,128]{3,2,1,0:T(2,128)S(1)} %get-tuple-element.11), channel_id=1, source_target_pairs={{2,0},{4,2},{6,4},{8,6},{10,8},{12,10},{14,12},{3,1},{5,3},{7,5},{... | collective-permute-start | bytes 196616 | tf_op jit(solution)/shard_map/ppermute | solution.py:272
  3.8 1.3 %collective-permute-start = (f32[8,8,2,128]{3,2,1,0:T(2,128)S(1)}, f32[8,8,2,128]{3,2,1,0:T(2,128)S(1)}, u32[]{:S(2)}, u32[]{:S(2)}) collective-permute-start(f32[8,8,2,128]{3,2,1,0:T(2,128)S(1)} %get-tuple-element.10), channel_id=1, source_target_pairs={{0,2},{2,4},{4,6},{6,8},{8,10},{10,12},{12,14},{1,3},{3,5},{5,7},{... | collective-permute-start | bytes 196616 | tf_op jit(solution)/shard_map/ppermute | solution.py:271
  5.1 1.9 %copy.31 = bf16[8,4,128,128]{3,0,2,1:T(8,128)(2,1)S(1)} copy(bf16[8,4,128,128]{3,2,1,0:T(8,128)(2,1)} %param.13) | data formatting | bytes 2097152 | tf_op args[0]
  7.1 0.0 copy-start.1
  7.1 0.1 pad_slice_fusion
  7.2 1.3 %collective-permute-start.2 = (bf16[2,1056,128]{2,1,0:T(8,128)(2,1)S(1)}, bf16[2,1056,128]{2,1,0:T(8,128)(2,1)S(1)}, u32[]{:S(2)}, u32[]{:S(2)}) collective-permute-start(bf16[2,1056,128]{2,1,0:T(8,128)(2,1)S(1)} %get-tuple-element.9), channel_id=1, source_target_pairs={{0,2},{2,4},{4,6},{6,8},{8,10},{10,12},{12,14},{1,3},{3,5},{5,7},{... | collective-permute-start | bytes 1622024 | tf_op jit(solution)/shard_map/ppermute | solution.py:279
  8.4 5.4 %collective-permute-start.3 = (bf16[2,1056,128]{2,1,0:T(8,128)(2,1)S(1)}, bf16[2,1056,128]{2,1,0:T(8,128)(2,1)}, u32[]{:S(2)}, u32[]{:S(2)}) collective-permute-start(bf16[2,1056,128]{2,1,0:T(8,128)(2,1)S(1)} %get-tuple-element.8), channel_id=1, source_target_pairs={{2,0},{4,2},{6,4},{8,6},{10,8},{12,10},{14,12},{3,1},{5,3},{7,5},{... | collective-permute-start | bytes 1622024 | tf_op jit(solution)/shard_map/ppermute | solution.py:280
  13.9 0.0 copy-done.1
  13.9 3.4 %collective-permute-start.4 = (f32[8,4,128]{2,1,0:T(4,128)S(1)}, f32[8,4,128]{2,1,0:T(4,128)S(1)}, u32[]{:S(2)}, u32[]{:S(2)}) collective-permute-start(f32[8,4,128]{2,1,0:T(4,128)S(1)} %slice_bitcast_fusion), channel_id=1, source_target_pairs={{1,0},{3,2},{5,4},{7,6},{9,8},{11,10},{13,12},{15,14},{17,16},{19,... | collective-permute-start | bytes 49160 | tf_op jit(solution)/shard_map/ppermute | solution.py:274
  17.3 0.5 and_convert_fusion.mask_ref
  17.8 1.3 %copy.25 = bf16[4,1024,128]{1,2,0:T(8,128)(2,1)} copy(bf16[4,1024,128]{2,1,0:T(8,128)(2,1)S(1)} %bitcast.27) | data formatting | bytes 2097152 | tf_op jit(solution)/shard_map/reshape | solution.py:276
  19.1 1.1 pad.4.own_ref
  20.3 0.0 collective-permute-done.1
  20.3 0.0 collective-permute-done
  20.3 0.1 maximum_bitcast_fusion
  20.4 3.1 %copy.22 = f32[8,128,8,8]{3,2,1,0:T(8,128)} copy(f32[8,128,8,8]{1,0,3,2:T(8,128)S(1)} %maximum_bitcast_fusion) | data formatting | bytes 524288 | tf_op jit(solution)/shard_map/transpose | solution.py:283
  23.5 13.1 %shard_map.140 = (f32[6,32,8,256]{3,2,1,0:T(8,128)}, f32[4,32,8,256]{3,2,1,0:T(8,128)}, f32[4,1024,8]{2,1,0:T(8,128)}) custom-call(f32[6]{0:T(128)} %and_convert_fusion.mask_ref, f32[8,1024,8]{2,1,0:T(8,128)} %bitcast.29, bf16[8,64]{1,0:T(8,128)(2,1)} %bitcast.38, bf16[8,64]{1,0:T(8,128)(2,1)} %bitcast.40, bf16[8,64]{1,0:T(8,128)(2,1)} %p1.3, ...), custom_call_target="tpu_custom_call" | custom-call | flops 100000000 | bytes 10000000 | tf_op jit(solution)/shard_map/pallas_call | solution.py:289
  36.6 0.0 slice-start
  36.6 0.0 copy-start
  36.6 2.3 %copy.23 = f32[4,128,8,8]{1,0,3,2:T(4,128)S(1)} copy(f32[4,128,8,8]{3,2,1,0:T(8,128)} %bitcast.30) | data formatting | bytes 262144 | tf_op jit(solution)/shard_map/reshape | solution.py:309
  38.8 0.0 copy-start.2
  38.8 0.0 collective-permute-done.4
  38.8 0.0 slice-done
  38.9 0.0 copy-done
  38.9 0.9 convolution_bitcast_fusion.vecs_ref
  39.8 0.0 collective-permute-done.2.low_ref
  39.8 0.0 copy-start.3
  39.8 0.0 collective-permute-done.3.high_ref
  39.8 0.8 copy-done.3
  40.6 41.3 %shard_map.141.mats_ref = f32[1024,128]{1,0:T(8,128)} custom-call(bf16[2,1056,128]{2,1,0:T(8,128)(2,1)} %copy-done.3, bf16[4,1056,128]{2,1,0:T(8,128)(2,1)} %pad.4.own_ref, bf16[2,1056,128]{2,1,0:T(8,128)(2,1)} %collective-permute-done.3.high_ref, bf16[4,128,1024]{2,1,0:T(8,128)(2,1)} %bitcast.31, f32[6,32,8,256]{3,2,1,0:T(8,128)} %get-tuple-element.6.s1_ref, ...), custom_call_target="tpu_custom_call" | custom-call | flops 20000000000 | bytes 10000000 | tf_op jit(solution)/shard_map/pallas_call | solution.py:315
  81.8 0.0 copy-done.2
  81.8 37.0 %shard_map.142 = f32[8,128]{1,0:T(8,128)} custom-call(f32[1024,128]{1,0:T(8,128)} %shard_map.141.mats_ref, f32[8,128]{1,0:T(8,128)} %convolution_bitcast_fusion.vecs_ref), custom_call_target="tpu_custom_call" | custom-call | tf_op jit(solution)/shard_map/pallas_call | solution.py:338
  118.9 1.3 %copy.33 = f32[8,128]{1,0:T(8,128)} copy(f32[8,128]{1,0:T(8,128)} %shard_map.142) | data formatting | bytes 8192
  (2 shorter events, 0.0 us)
Async XLA Ops:
  1.7 18.6 %collective-permute-start.1 = (f32[8,8,2,128]{3,2,1,0:T(2,128)S(1)}, f32[8,8,2,128]{3,2,1,0:T(2,128)S(1)}, u32[]{:S(2)}, u32[]{:S(2)}) collective-permute-start(f32[8,8,2,128]{3,2,1,0:T(2,128)S(1)} %get-tuple-element.11), channel_id=1, source_target_pairs={{2,0},{4,2},{6,4},{8,6},{10,8},{12,10},{14,12},{3,1},{5,3},{7,5},{... | collective-permute-start | bytes 196616 | tf_op jit(solution)/shard_map/ppermute | solution.py:272
  3.8 16.4 %collective-permute-start = (f32[8,8,2,128]{3,2,1,0:T(2,128)S(1)}, f32[8,8,2,128]{3,2,1,0:T(2,128)S(1)}, u32[]{:S(2)}, u32[]{:S(2)}) collective-permute-start(f32[8,8,2,128]{3,2,1,0:T(2,128)S(1)} %get-tuple-element.10), channel_id=1, source_target_pairs={{0,2},{2,4},{4,6},{6,8},{8,10},{10,12},{12,14},{1,3},{3,5},{5,7},{... | collective-permute-start | bytes 196616 | tf_op jit(solution)/shard_map/ppermute | solution.py:271
  7.1 6.8 %copy-start.1 = (f32[8,8,4,128]{3,2,1,0:T(4,128)S(1)}, f32[8,8,4,128]{3,2,1,0:T(4,128)}, u32[]{:S(2)}) copy-start(f32[8,8,4,128]{3,2,1,0:T(4,128)} %param.14) | copy-start | bytes 393220
  7.2 32.6 %collective-permute-start.2 = (bf16[2,1056,128]{2,1,0:T(8,128)(2,1)S(1)}, bf16[2,1056,128]{2,1,0:T(8,128)(2,1)S(1)}, u32[]{:S(2)}, u32[]{:S(2)}) collective-permute-start(bf16[2,1056,128]{2,1,0:T(8,128)(2,1)S(1)} %get-tuple-element.9), channel_id=1, source_target_pairs={{0,2},{2,4},{4,6},{6,8},{8,10},{10,12},{12,14},{1,3},{3,5},{5,7},{... | collective-permute-start | bytes 1622024 | tf_op jit(solution)/shard_map/ppermute | solution.py:279
  8.4 31.3 %collective-permute-start.3 = (bf16[2,1056,128]{2,1,0:T(8,128)(2,1)S(1)}, bf16[2,1056,128]{2,1,0:T(8,128)(2,1)}, u32[]{:S(2)}, u32[]{:S(2)}) collective-permute-start(bf16[2,1056,128]{2,1,0:T(8,128)(2,1)S(1)} %get-tuple-element.8), channel_id=1, source_target_pairs={{2,0},{4,2},{6,4},{8,6},{10,8},{12,10},{14,12},{3,1},{5,3},{7,5},{... | collective-permute-start | bytes 1622024 | tf_op jit(solution)/shard_map/ppermute | solution.py:280
  13.9 24.9 %collective-permute-start.4 = (f32[8,4,128]{2,1,0:T(4,128)S(1)}, f32[8,4,128]{2,1,0:T(4,128)S(1)}, u32[]{:S(2)}, u32[]{:S(2)}) collective-permute-start(f32[8,4,128]{2,1,0:T(4,128)S(1)} %slice_bitcast_fusion), channel_id=1, source_target_pairs={{1,0},{3,2},{5,4},{7,6},{9,8},{11,10},{13,12},{15,14},{17,16},{19,... | collective-permute-start | bytes 49160 | tf_op jit(solution)/shard_map/ppermute | solution.py:274
  36.6 2.3 %slice-start = ((f32[8,8,4,128]{3,2,1,0:T(4,128)}), f32[7,8,4,128]{3,2,1,0:T(4,128)S(1)}, s32[]{:S(2)}) async-start(f32[8,8,4,128]{3,2,1,0:T(4,128)} %param.14), calls=%async_computation | async-start | bytes 229376 | tf_op jit(solution)/shard_map/slice | solution.py:310
  36.6 2.3 %copy-start = (bf16[8,4,128,128]{3,2,1,0:T(8,128)(2,1)S(1)}, bf16[8,4,128,128]{3,2,1,0:T(8,128)(2,1)}, u32[]{:S(2)}) copy-start(bf16[8,4,128,128]{3,2,1,0:T(8,128)(2,1)} %param.13) | copy-start | bytes 3145732
  38.8 43.0 %copy-start.2 = (f32[4,128,8,8]{1,0,3,2:T(4,128)}, f32[4,128,8,8]{1,0,3,2:T(4,128)S(1)}, u32[]{:S(2)}) copy-start(f32[4,128,8,8]{1,0,3,2:T(4,128)S(1)} %copy.23) | copy-start | bytes 393220
  39.8 0.8 copy-start.3

commit v5 on v4

--- a/solution.py
+++ b/solution.py
@@ -47,7 +47,7 @@
     z2_ref[:, 0:8, :] = edge2
     z2_ref[:, span + 8 : span + 16, :] = edge2
 
-    @pl.loop(0, rows + 4, unroll=4)
+    @pl.loop(0, rows + 4, unroll=8)
     def _(r):
         z_ref[r, 8 : span + 8, :] = dot_split(u_ref[r], l1[...])
 
@@ -61,7 +61,7 @@
                 acc = acc + taps[3 * i + j : 3 * i + j + 1, :] * ref[r + i, pl.ds(base + 8 * j, size), :]
         return jnp.tanh(acc)
 
-    @pl.loop(0, (rows + 2) * pieces, unroll=4)
+    @pl.loop(0, (rows + 2) * pieces, unroll=8)
     def _(n):
         r, q = n // pieces, n % pieces
         base = pl.multiple_of(q * size, size)
@@ -72,7 +72,7 @@
         m_ref[r, pl.ds(base, size), :] = mid
         z2_ref[r, pl.ds(base + 8, size), :] = dot_split(mid, l2[...])
 
-    @pl.loop(0, rows * pieces, unroll=4)
+    @pl.loop(0, rows * pieces, unroll=8)
     def _(n):
         r, q = n // pieces, n % pieces
         base = pl.multiple_of(q * size, size)
@@ -109,7 +109,7 @@
         lhs = jnp.concatenate([(slopes[s : s + 1, :] * scale).astype(BF16) for s in range(segs)], axis=0)
         return dot(lhs, k_ref[h]).astype(BF16)
 
-    @pl.loop(0, (rows + 2) * tiles, unroll=8)
+    @pl.loop(0, (rows + 2) * tiles, unroll=16)
     def _(n):
         r, t = n // tiles, n % tiles
         at = pl.multiple_of(t * 64, 64)
@@ -124,7 +124,7 @@
 
     @pl.loop(0, rows)
     def _(r):
-        @pl.loop(0, tiles, unroll=8)
+        @pl.loop(0, tiles, unroll=16)
         def _(t):
             at = pl.multiple_of(t * 64, 64)
             bands = [band(s2_ref[r, 2 * t + h], pd2, k2_ref, h) for h in range(2)]

time: 120 us -> 116 us (0.967)
  Pallas kernels: 91.3 us -> 86.7 us
    pallas_call x1, Pallas kernels: 41.3 us -> 38.1 us  [on_device(): pl.pallas_call(functools.partial(tangent_kernel, rows, segs), out_shape=j...]
    pallas_call x1, Pallas kernels: 13.1 us -> 11.7 us  [on_device(): pl.pallas_call(functools.partial(advance_kernel, rows), out_shape=(jax.Sh...]
  transfers between devices with their start and end apart: 5 -> 5, of which waited for: 0 -> 0; matrix products, arithmetic and copies ran while one was open for 9% -> 10% of each run, Pallas kernels for 11% -> 10%
where the time goes in v5:
time: 116 us
  Pallas kernels  86.7 us (75%)
  starting transfers between devices  13.6 us (12%)
  local copies, waits for them, and re-layouts  12.9 us (11%)
    pallas_call x1, Pallas kernels, on_device(): pl.pallas_call(functools.partial(tangent_kernel, rows, segs), out_shape=j...  38.1 us
    pallas_call x1, Pallas kernels, on_device(): pl.pallas_call(functools.partial(close_kernel, segs, count, turns), out_s...  37 us
    pallas_call x1, Pallas kernels, on_device(): pl.pallas_call(functools.partial(advance_kernel, rows), out_shape=(jax.Sh...  11.7 us
    ppermute x1, starting transfers between devices, on_device(): high = lax.ppermute(own[:2], 'space', up)  5.42 us
    unnamed x10, local copies, waits for them, and re-layouts  3.98 us
    ppermute x1, starting transfers between devices, on_device(): lax.ppermute(states[0], 'seg', [(i + 1, i) for i in range(turns - 1)])  3.41 us
    transpose x1, local copies, waits for them, and re-layouts, on_device(): jnp.transpose(extended, (2, 3, 0, 1)).reshape(rows + 4, cols * segs, fields)  3.11 us
  transfers between devices with their start and end apart: 5, of which 0 were waited for; matrix products, arithmetic and copies ran while one was open for 10% of the time, Pallas kernels for 10%

profile of v5, /device:TPU:31, one launch (start us, length us, event | category | flops | bytes accessed | tf_op | source)
XLA Modules:
  0.0 115.5 jit_solution(133444776296557315)
XLA Ops:
  0.6 1.0 fusion.2
  1.7 2.2 %collective-permute-start.1 = (f32[8,8,2,128]{3,2,1,0:T(2,128)S(1)}, f32[8,8,2,128]{3,2,1,0:T(2,128)S(1)}, u32[]{:S(2)}, u32[]{:S(2)}) collective-permute-start(f32[8,8,2,128]{3,2,1,0:T(2,128)S(1)} %get-tuple-element.11), channel_id=1, source_target_pairs={{2,0},{4,2},{6,4},{8,6},{10,8},{12,10},{14,12},{3,1},{5,3},{7,5},{... | collective-permute-start | bytes 196616 | tf_op jit(solution)/shard_map/ppermute | solution.py:272
  3.8 1.3 %collective-permute-start = (f32[8,8,2,128]{3,2,1,0:T(2,128)S(1)}, f32[8,8,2,128]{3,2,1,0:T(2,128)S(1)}, u32[]{:S(2)}, u32[]{:S(2)}) collective-permute-start(f32[8,8,2,128]{3,2,1,0:T(2,128)S(1)} %get-tuple-element.10), channel_id=1, source_target_pairs={{0,2},{2,4},{4,6},{6,8},{8,10},{10,12},{12,14},{1,3},{3,5},{5,7},{... | collective-permute-start | bytes 196616 | tf_op jit(solution)/shard_map/ppermute | solution.py:271
  5.1 1.9 %copy.31 = bf16[8,4,128,128]{3,0,2,1:T(8,128)(2,1)S(1)} copy(bf16[8,4,128,128]{3,2,1,0:T(8,128)(2,1)} %param.13) | data formatting | bytes 2097152 | tf_op args[0]
  7.1 0.0 copy-start.1
  7.1 0.1 pad_slice_fusion
  7.2 1.3 %collective-permute-start.2 = (bf16[2,1056,128]{2,1,0:T(8,128)(2,1)S(1)}, bf16[2,1056,128]{2,1,0:T(8,128)(2,1)S(1)}, u32[]{:S(2)}, u32[]{:S(2)}) collective-permute-start(bf16[2,1056,128]{2,1,0:T(8,128)(2,1)S(1)} %get-tuple-element.9), channel_id=1, source_target_pairs={{0,2},{2,4},{4,6},{6,8},{8,10},{10,12},{12,14},{1,3},{3,5},{5,7},{... | collective-permute-start | bytes 1622024 | tf_op jit(solution)/shard_map/ppermute | solution.py:279
  8.4 5.4 %collective-permute-start.3 = (bf16[2,1056,128]{2,1,0:T(8,128)(2,1)S(1)}, bf16[2,1056,128]{2,1,0:T(8,128)(2,1)}, u32[]{:S(2)}, u32[]{:S(2)}) collective-permute-start(bf16[2,1056,128]{2,1,0:T(8,128)(2,1)S(1)} %get-tuple-element.8), channel_id=1, source_target_pairs={{2,0},{4,2},{6,4},{8,6},{10,8},{12,10},{14,12},{3,1},{5,3},{7,5},{... | collective-permute-start | bytes 1622024 | tf_op jit(solution)/shard_map/ppermute | solution.py:280
  13.9 0.0 copy-done.1
  13.9 3.4 %collective-permute-start.4 = (f32[8,4,128]{2,1,0:T(4,128)S(1)}, f32[8,4,128]{2,1,0:T(4,128)S(1)}, u32[]{:S(2)}, u32[]{:S(2)}) collective-permute-start(f32[8,4,128]{2,1,0:T(4,128)S(1)} %slice_bitcast_fusion), channel_id=1, source_target_pairs={{1,0},{3,2},{5,4},{7,6},{9,8},{11,10},{13,12},{15,14},{17,16},{19,... | collective-permute-start | bytes 49160 | tf_op jit(solution)/shard_map/ppermute | solution.py:274
  17.3 0.5 and_convert_fusion.mask_ref
  17.8 1.3 %copy.25 = bf16[4,1024,128]{1,2,0:T(8,128)(2,1)} copy(bf16[4,1024,128]{2,1,0:T(8,128)(2,1)S(1)} %bitcast.27) | data formatting | bytes 2097152 | tf_op jit(solution)/shard_map/reshape | solution.py:276
  19.1 1.1 pad.4.own_ref
  20.3 0.0 collective-permute-done.1
  20.3 0.0 collective-permute-done
  20.3 0.1 maximum_bitcast_fusion
  20.4 3.1 %copy.22 = f32[8,128,8,8]{3,2,1,0:T(8,128)} copy(f32[8,128,8,8]{1,0,3,2:T(8,128)S(1)} %maximum_bitcast_fusion) | data formatting | bytes 524288 | tf_op jit(solution)/shard_map/transpose | solution.py:283
  23.5 11.7 %shard_map.140 = (f32[6,32,8,256]{3,2,1,0:T(8,128)}, f32[4,32,8,256]{3,2,1,0:T(8,128)}, f32[4,1024,8]{2,1,0:T(8,128)}) custom-call(f32[6]{0:T(128)} %and_convert_fusion.mask_ref, f32[8,1024,8]{2,1,0:T(8,128)} %bitcast.29, bf16[8,64]{1,0:T(8,128)(2,1)} %bitcast.38, bf16[8,64]{1,0:T(8,128)(2,1)} %bitcast.40, bf16[8,64]{1,0:T(8,128)(2,1)} %p1.3, ...), custom_call_target="tpu_custom_call" | custom-call | flops 100000000 | bytes 10000000 | tf_op jit(solution)/shard_map/pallas_call | solution.py:289
  35.2 0.0 slice-start
  35.2 0.0 copy-start
  35.2 2.3 %copy.23 = f32[4,128,8,8]{1,0,3,2:T(4,128)S(1)} copy(f32[4,128,8,8]{3,2,1,0:T(8,128)} %bitcast.30) | data formatting | bytes 262144 | tf_op jit(solution)/shard_map/reshape | solution.py:309
  37.4 0.0 copy-start.2
  37.4 0.0 collective-permute-done.4
  37.4 0.0 slice-done
  37.5 0.0 copy-done
  37.5 0.9 convolution_bitcast_fusion.vecs_ref
  38.4 0.0 collective-permute-done.2.low_ref
  38.4 0.0 copy-start.3
  38.4 0.0 collective-permute-done.3.high_ref
  38.4 0.8 copy-done.3
  39.2 38.1 %shard_map.141.mats_ref = f32[1024,128]{1,0:T(8,128)} custom-call(bf16[2,1056,128]{2,1,0:T(8,128)(2,1)} %copy-done.3, bf16[4,1056,128]{2,1,0:T(8,128)(2,1)} %pad.4.own_ref, bf16[2,1056,128]{2,1,0:T(8,128)(2,1)} %collective-permute-done.3.high_ref, bf16[4,128,1024]{2,1,0:T(8,128)(2,1)} %bitcast.31, f32[6,32,8,256]{3,2,1,0:T(8,128)} %get-tuple-element.6.s1_ref, ...), custom_call_target="tpu_custom_call" | custom-call | flops 20000000000 | bytes 10000000 | tf_op jit(solution)/shard_map/pallas_call | solution.py:315
  77.3 0.0 copy-done.2
  77.3 37.0 %shard_map.142 = f32[8,128]{1,0:T(8,128)} custom-call(f32[1024,128]{1,0:T(8,128)} %shard_map.141.mats_ref, f32[8,128]{1,0:T(8,128)} %convolution_bitcast_fusion.vecs_ref), custom_call_target="tpu_custom_call" | custom-call | tf_op jit(solution)/shard_map/pallas_call | solution.py:338
  114.2 1.3 %copy.33 = f32[8,128]{1,0:T(8,128)} copy(f32[8,128]{1,0:T(8,128)} %shard_map.142) | data formatting | bytes 8192
  (2 shorter events, 0.0 us)
Async XLA Ops:
  1.7 18.6 %collective-permute-start.1 = (f32[8,8,2,128]{3,2,1,0:T(2,128)S(1)}, f32[8,8,2,128]{3,2,1,0:T(2,128)S(1)}, u32[]{:S(2)}, u32[]{:S(2)}) collective-permute-start(f32[8,8,2,128]{3,2,1,0:T(2,128)S(1)} %get-tuple-element.11), channel_id=1, source_target_pairs={{2,0},{4,2},{6,4},{8,6},{10,8},{12,10},{14,12},{3,1},{5,3},{7,5},{... | collective-permute-start | bytes 196616 | tf_op jit(solution)/shard_map/ppermute | solution.py:272
  3.8 16.4 %collective-permute-start = (f32[8,8,2,128]{3,2,1,0:T(2,128)S(1)}, f32[8,8,2,128]{3,2,1,0:T(2,128)S(1)}, u32[]{:S(2)}, u32[]{:S(2)}) collective-permute-start(f32[8,8,2,128]{3,2,1,0:T(2,128)S(1)} %get-tuple-element.10), channel_id=1, source_target_pairs={{0,2},{2,4},{4,6},{6,8},{8,10},{10,12},{12,14},{1,3},{3,5},{5,7},{... | collective-permute-start | bytes 196616 | tf_op jit(solution)/shard_map/ppermute | solution.py:271
  7.1 6.8 %copy-start.1 = (f32[8,8,4,128]{3,2,1,0:T(4,128)S(1)}, f32[8,8,4,128]{3,2,1,0:T(4,128)}, u32[]{:S(2)}) copy-start(f32[8,8,4,128]{3,2,1,0:T(4,128)} %param.14) | copy-start | bytes 393220
  7.2 31.2 %collective-permute-start.2 = (bf16[2,1056,128]{2,1,0:T(8,128)(2,1)S(1)}, bf16[2,1056,128]{2,1,0:T(8,128)(2,1)S(1)}, u32[]{:S(2)}, u32[]{:S(2)}) collective-permute-start(bf16[2,1056,128]{2,1,0:T(8,128)(2,1)S(1)} %get-tuple-element.9), channel_id=1, source_target_pairs={{0,2},{2,4},{4,6},{6,8},{8,10},{10,12},{12,14},{1,3},{3,5},{5,7},{... | collective-permute-start | bytes 1622024 | tf_op jit(solution)/shard_map/ppermute | solution.py:279
  8.4 30.0 %collective-permute-start.3 = (bf16[2,1056,128]{2,1,0:T(8,128)(2,1)S(1)}, bf16[2,1056,128]{2,1,0:T(8,128)(2,1)}, u32[]{:S(2)}, u32[]{:S(2)}) collective-permute-start(bf16[2,1056,128]{2,1,0:T(8,128)(2,1)S(1)} %get-tuple-element.8), channel_id=1, source_target_pairs={{2,0},{4,2},{6,4},{8,6},{10,8},{12,10},{14,12},{3,1},{5,3},{7,5},{... | collective-permute-start | bytes 1622024 | tf_op jit(solution)/shard_map/ppermute | solution.py:280
  13.9 23.6 %collective-permute-start.4 = (f32[8,4,128]{2,1,0:T(4,128)S(1)}, f32[8,4,128]{2,1,0:T(4,128)S(1)}, u32[]{:S(2)}, u32[]{:S(2)}) collective-permute-start(f32[8,4,128]{2,1,0:T(4,128)S(1)} %slice_bitcast_fusion), channel_id=1, source_target_pairs={{1,0},{3,2},{5,4},{7,6},{9,8},{11,10},{13,12},{15,14},{17,16},{19,... | collective-permute-start | bytes 49160 | tf_op jit(solution)/shard_map/ppermute | solution.py:274
  35.2 2.3 %slice-start = ((f32[8,8,4,128]{3,2,1,0:T(4,128)}), f32[7,8,4,128]{3,2,1,0:T(4,128)S(1)}, s32[]{:S(2)}) async-start(f32[8,8,4,128]{3,2,1,0:T(4,128)} %param.14), calls=%async_computation | async-start | bytes 229376 | tf_op jit(solution)/shard_map/slice | solution.py:310
  35.2 2.3 %copy-start = (bf16[8,4,128,128]{3,2,1,0:T(8,128)(2,1)S(1)}, bf16[8,4,128,128]{3,2,1,0:T(8,128)(2,1)}, u32[]{:S(2)}) copy-start(bf16[8,4,128,128]{3,2,1,0:T(8,128)(2,1)} %param.13) | copy-start | bytes 3145732
  37.4 39.8 %copy-start.2 = (f32[4,128,8,8]{1,0,3,2:T(4,128)}, f32[4,128,8,8]{1,0,3,2:T(4,128)S(1)}, u32[]{:S(2)}) copy-start(f32[4,128,8,8]{1,0,3,2:T(4,128)S(1)} %copy.23) | copy-start | bytes 393220
  38.4 0.8 copy-start.3
